TPU v7x, 256 devices: a whole 4x4x8 slice. The times are simulated.
256 devices in a mesh: ctx: 16 (over y_hi, x, core), mp: 16 (over y_lo, z).
Axes of the slice: x: 4, y: 4 (y_hi: 2, y_lo: 2; y = y_hi * 2 + y_lo), z: 8, core: 2. Of those that a mesh axis runs over, the one named last changes fastest.
Arguments:
- token_ids: int32 [12288], P('ctx'), may hold values from 0 to 511
- feature_table: bfloat16 [512, 3, 4096], P(None, None, 'mp'), may hold values from -6 to 6
- short_filter: float32 [3, 3, 4096], P(None, None, 'mp'), may hold values from -4 to 4
- rates: float32 [4096, 16], P('mp'), may hold values from 1 to 384
- residues: float32 [4096, 16], P('mp'), may hold values from -1.5 to 1.5
- skip_weight: float32 [4096], P('mp'), may hold values from -4 to 4
- w_qkv: bfloat16 [4096, 3, 4096], P(None, None, 'mp'), may hold values from -2 to 2
Outputs:
- hyena_out: bfloat16 [12288, 4096], P('ctx', 'mp')
- attended: bfloat16 [12288, 4096], P('ctx', 'mp')
All inputs are finite; a program needn't handle non-finite values.
Results may differ from a plain program's by a relative error of at most 0.039.
The roundings to bfloat16 on the way count: a program that leaves them out, or rounds other values in their place, can miss the bound.
Values may be sent and summed in bfloat16 or wider, within the bound.
A program may use at most 128 MiB of HBM per device.

v0:
```python
import math

import jax
import jax.numpy as jnp
import numpy as np
from jax import lax
from jax.sharding import PartitionSpec as P

HEAD_DIM = 128
TAPS = 3


NEG_FILL = -1e30
NORM_EPSILON = 1e-06


def passed_along(block, axis, distance):
    devices = range(lax.axis_size(axis))
    route = [(i - distance, i) for i in devices if i - distance in devices]
    return lax.ppermute(block, axis, route)


def entering(part, axis, combine, identity):
    place = lax.axis_index(axis)
    gathered = jax.tree.map(lambda a: lax.all_gather(a, axis), part)
    state = jax.tree.map(lambda a, e: jnp.zeros_like(a) + jnp.asarray(e, a.dtype), part, identity)

    def one(hop, state):
        return combine(
            state, jax.tree.map(lambda a: lax.dynamic_index_in_dim(a, hop, 0, False), gathered)
        )

    return lax.fori_loop(0, place, one, state)


def lookup_rows(token_ids, feature_table):
    vocab_size = feature_table.shape[0]
    one_hot = (token_ids[:, None] == jnp.arange(vocab_size, dtype=jnp.int32)[None, :]).astype(
        jnp.bfloat16
    )
    looked = jnp.dot(
        one_hot, feature_table.reshape(vocab_size, -1), preferred_element_type=jnp.float32
    )
    return looked.reshape(token_ids.shape[0], 3, feature_table.shape[2])


def chain_combine(earlier, later):
    return (earlier[0] * later[0], later[0] * earlier[1] + later[1])


def empty_state(query_len, heads_dev, head_size):
    return (
        jnp.full((heads_dev, query_len), NEG_FILL, jnp.float32),
        jnp.zeros((heads_dev, query_len), jnp.float32),
        jnp.zeros((query_len, heads_dev, head_size), jnp.float32),
    )


def attend(carried, queries, query_pos, key_rows, value_rows, key_pos):
    highest, totals, summed = carried
    scale = 1.0 / math.sqrt(queries.shape[-1])
    scores = (
        jnp.einsum("qhd,khd->hqk", queries, key_rows, preferred_element_type=jnp.float32) * scale
    )
    allowed = (key_pos[None, :] <= query_pos[:, None])[None, :, :]
    scores = jnp.where(allowed, scores, NEG_FILL)
    new_high = jnp.maximum(highest, jnp.max(scores, axis=2))
    shrink = jnp.exp(highest - new_high)
    weights = jnp.where(allowed, jnp.exp(scores - new_high[:, :, None]), 0.0)
    totals = totals * shrink + jnp.sum(weights, axis=2)
    update = jnp.einsum(
        "hqk,khd->qhd", weights.astype(jnp.bfloat16), value_rows, preferred_element_type=jnp.float32
    )
    summed = summed * jnp.transpose(shrink)[:, :, None] + update
    return (new_high, totals, summed)


def finish(carried):
    highest, totals, summed = carried
    result = summed / jnp.transpose(totals)[:, :, None]
    return result.reshape(summed.shape[0], -1).astype(jnp.bfloat16)


def key_fold_for(query_sets, key_len, carried, portion):
    key_rows, value_rows = portion
    shard_count = key_rows.shape[0] // key_len

    def per_shard(number, inner):
        offset = number * key_len
        block_keys = lax.dynamic_slice_in_dim(key_rows, offset, key_len, 0)
        block_values = lax.dynamic_slice_in_dim(value_rows, offset, key_len, 0)
        key_pos = offset + jnp.arange(key_len, dtype=jnp.int32)
        queries, query_pos, last_pos = query_sets[0]

        def run_it(current):
            return attend(current, queries, query_pos, block_keys, block_values, key_pos)

        def keep_it(current):
            return current

        updated = [lax.cond(offset <= last_pos, run_it, keep_it, inner[0])]
        return tuple(updated)

    return lax.fori_loop(0, shard_count, per_shard, carried)


def per_device(token_ids, feature_table, short_filter, rates, residues, skip_weight, w_qkv):
    rows = token_ids.shape[0]
    channels = feature_table.shape[2]
    ctx_size = lax.axis_size("ctx")
    my_index = lax.axis_index("ctx")
    seq_total = rows * ctx_size
    features = lookup_rows(token_ids, feature_table)
    rim_ids = passed_along(token_ids[rows - (TAPS - 1) :], "ctx", 1)
    rim_rows = lookup_rows(rim_ids, feature_table) * (my_index > 0).astype(jnp.float32)
    extended = jnp.concatenate([rim_rows, features], axis=0)
    smoothed = short_filter[0][None] * extended[TAPS - 1 : TAPS - 1 + rows]
    for tap_index in range(1, TAPS):
        smoothed = (
            smoothed
            + short_filter[tap_index][None]
            * extended[TAPS - 1 - tap_index : TAPS - 1 - tap_index + rows]
        )
    gate_prod = smoothed[:, 1] * smoothed[:, 2]
    damping = rates / seq_total
    mode_weight = residues * jnp.sqrt(-jnp.expm1(-2.0 * damping))
    block_len = math.gcd(rows, 128)
    block_count = rows // block_len
    steps_in = jnp.arange(block_len, dtype=jnp.float32)
    lagged = jnp.exp(-damping[:, :, None] * steps_in[None, None, :])
    rising = jnp.exp(-damping[:, :, None] * (steps_in[None, None, :] + 1.0))
    falling = jnp.exp(-damping[:, :, None] * (block_len - 1.0 - steps_in[None, None, :]))
    kernel = jnp.einsum("cr,crt->ct", mode_weight, lagged, precision=lax.Precision.HIGHEST)
    lag_index = np.arange(block_len)[:, None] - np.arange(block_len)[None, :]
    toeplitz = jnp.where(
        jnp.asarray(lag_index >= 0)[None], kernel[:, np.maximum(lag_index, 0)], 0.0
    )
    gate_blocks = gate_prod.reshape(block_count, block_len, channels)
    inside = jnp.einsum("cts,bsc->btc", toeplitz, gate_blocks, precision=lax.Precision.HIGHEST)
    block_ends = jnp.einsum("crs,bsc->bcr", falling, gate_blocks, precision=lax.Precision.HIGHEST)
    block_decay = jnp.exp(-damping * block_len)

    def advance(carried, block_end):
        return (block_decay * carried + block_end, carried)

    device_end, block_starts = lax.scan(advance, jnp.zeros_like(damping), block_ends)
    device_decay = jnp.exp(-damping * rows)
    scanned = entering(
        (device_decay, device_end),
        "ctx",
        chain_combine,
        (jnp.ones_like(damping), jnp.zeros_like(damping)),
    )
    incoming = scanned[1]
    offsets = (block_len * jnp.arange(block_count, dtype=jnp.int32)).astype(jnp.float32)
    powers = jnp.exp(-damping[None] * offsets[:, None, None])
    true_starts = block_starts + powers * incoming[None]
    carried_in = jnp.einsum(
        "crt,bcr->btc",
        mode_weight[:, :, None] * rising,
        true_starts,
        precision=lax.Precision.HIGHEST,
    )
    convolved = (inside + carried_in).reshape(rows, channels)
    hyena_out = (smoothed[:, 0] * (convolved + skip_weight[None, :] * gate_prod)).astype(
        jnp.bfloat16
    )
    all_channels = w_qkv.shape[0]
    head_width = w_qkv.shape[2]
    portion = lax.all_gather(hyena_out, "mp", axis=1, tiled=True)
    summed = jnp.einsum("lc,cjf->ljf", portion, w_qkv, preferred_element_type=jnp.float32)
    widened = portion.astype(jnp.float32)
    squares = jnp.sum(widened * widened, axis=1)
    summed, squares = (summed, squares)
    projected = summed * lax.rsqrt(squares / all_channels + NORM_EPSILON)[:, None, None]
    heads_dev = head_width // HEAD_DIM
    queries = projected[:, 0].astype(jnp.bfloat16).reshape(rows, heads_dev, HEAD_DIM)
    key_rows = projected[:, 1].astype(jnp.bfloat16).reshape(rows, heads_dev, HEAD_DIM)
    value_rows = projected[:, 2].astype(jnp.bfloat16).reshape(rows, heads_dev, HEAD_DIM)
    own_pos = my_index * rows + jnp.arange(rows, dtype=jnp.int32)
    query_sets = [(queries, own_pos, my_index * rows + rows - 1)]
    result = key_fold_for(
        query_sets,
        rows,
        (empty_state(rows, heads_dev, HEAD_DIM),),
        (
            lax.all_gather(key_rows, "ctx", axis=0, tiled=True),
            lax.all_gather(value_rows, "ctx", axis=0, tiled=True),
        ),
    )
    attended = finish(result[0])
    return (hyena_out, attended)


def solution(mesh):
    in_specs = (
        P("ctx"),
        P(None, None, "mp"),
        P(None, None, "mp"),
        P("mp", None),
        P("mp", None),
        P("mp"),
        P(None, None, "mp"),
    )
    out_specs = (P("ctx", "mp"), P("ctx", "mp"))
    return jax.shard_map(
        per_device, mesh=mesh, in_specs=in_specs, out_specs=out_specs, check_vma=False
    )
```

profile of v0, /device:TPU:31, one launch (start us, length us, event | category | flops | bytes accessed | tf_op | source)
XLA Modules:
  0.0 592.1 jit_solution(12902735163480547101)
XLA Ops:
  12.4 2.9 fusion.47
  18.0 62.0 %gather_fusion = f32[16384,256]{1,0:T(8,128)} fusion(f32[256,128]{0,1:T(8,128)S(1)} %copy.49, s32[16384]{0:T(1024)S(1)} %broadcast_clamp_fusion), kind=kCustom, calls=%fused_computation | custom fusion | bytes 33619968 | tf_op jit(solution)/shard_map/gather | solution.py:136
  80.1 18.1 %copy.31 = f32[128,128,256]{1,0,2:T(8,128)} copy(f32[128,128,256]{2,1,0:T(8,128)} %bitcast.115) | data formatting | bytes 33554432 | tf_op jit(solution)/shard_map/gather | solution.py:136
  98.1 19.9 %all-gather = f32[4096,16]{0,1:T(8,128)S(1)} all-gather(f32[256,16]{0,1:T(8,128)S(1)} %get-tuple-element.490), channel_id=2, replica_groups=mesh['ctx'=16,'mp'=16] {'ctx'}, dimensions={0}, use_global_device_ids=true | all-gather | bytes 278528 | tf_op jit(solution)/shard_map/all_gather | solution.py:25
  119.1 3.8 fusion.35
  125.5 5.3 fusion.49
  132.3 3.7 while.45
  136.0 22.5 %all-gather.1 = f32[4096,16]{0,1:T(8,128)S(1)} all-gather(f32[256,16]{0,1:T(8,128)S(1)} %get-tuple-element.354), channel_id=3, replica_groups=mesh['ctx'=16,'mp'=16] {'ctx'}, dimensions={0}, use_global_device_ids=true | all-gather | bytes 278528 | tf_op jit(solution)/shard_map/all_gather | solution.py:25
  159.3 15.7 %while.43 = (s32[]{:T(128)}, f32[256,16]{0,1:T(8,128)S(1)}, s32[]{:T(128)}, f32[16,256,16]{1,0,2:T(8,128)}, f32[16,256,16]{1,0,2:T(8,128)}, /*index=5*/s32[]{:T(128)}, s32[]{:T(128)}, s32[]{:T(128)}) while((s32[]{:T(128)}, f32[256,16]{0,1:T(8,128)S(1)}, s32[]{:T(128)}, f32[16,256,16]{1,0,2:T(8,128)}, f32[16,256,16]{1,0,2:T(8,128)}, ...), condition=%wide.region_3.4_spmd, body=%wide.region_2.3_spmd.sunk | while | flops 8197 | bytes 131203 | solution.py:33
  177.3 28.7 %fusion.25 = f32[256,6,128]{2,1,0:T(8,128)S(1)} fusion(f32[6,128,256]{1,0,2:T(8,128)S(1)} %copy.32, f32[128,128,256]{1,0,2:T(8,128)} %copy.31, pred[128,128]{1,0:T(8,128)(4,1)} %bitcast.125), kind=kOutput, calls=%fused_computation.33 | convolution fusion | flops 306184192 | bytes 18366464 | tf_op jit(solution)/shard_map/cts,bsc->btc/dot_general | solution.py:139
  206.1 3.7 fusion.55
  212.3 97.7 %all-gather.6.cloned.1.call-done = bf16[768,4096]{1,0:T(8,128)(2,1)} async-done(((bf16[768,256]{1,0:T(8,128)(2,1)}), bf16[768,4096]{1,0:T(8,128)(2,1)}) %all-gather.6.cloned.1.call-update) | async-done | bytes 6291472 | tf_op jit(solution)/shard_map/all_gather | solution.py:170
  310.0 4.2 multiply_reduce_fusion
  314.6 7.6 %multiply_convert_fusion = bf16[768,3,256]{0,2,1:T(8,128)(2,1)S(1)} fusion(bf16[4096,3,256]{2,0,1:T(8,128)(2,1)} %param.24, bf16[768,4096]{1,0:T(8,128)(2,1)S(1)} %copy-done, f32[768]{0:T(1024)S(1)} %add_rsqrt_fusion), kind=kOutput, calls=%fused_computation.49 | convolution fusion | flops 4833017856 | bytes 13765632 | tf_op jit(solution)/shard_map/lc,cjf->ljf/dot_general | solution.py:171
  324.7 74.8 %all-gather.8.cloned.1.call-done = bf16[12288,2,128]{2,0,1:T(8,128)(2,1)} async-done(((bf16[768,2,128]{2,0,1:T(8,128)(2,1)}), bf16[12288,2,128]{2,0,1:T(8,128)(2,1)}) %all-gather.8.cloned.1.call-update) | async-done | bytes 6291472 | tf_op jit(solution)/shard_map/all_gather | solution.py:187
  399.5 70.6 %all-gather.10.cloned.1.call-done = bf16[12288,2,128]{2,0,1:T(8,128)(2,1)} async-done(((bf16[768,2,128]{2,0,1:T(8,128)(2,1)}), bf16[12288,2,128]{2,0,1:T(8,128)(2,1)}) %all-gather.10.cloned.1.call-update) | async-done | bytes 6291472 | tf_op jit(solution)/shard_map/all_gather | solution.py:188
  470.2 114.4 %while.44 = (s32[]{:T(128)}, f32[2,768]{1,0:T(2,128)S(1)}, f32[2,768]{1,0:T(2,128)S(1)}, f32[768,2,128]{2,0,1:T(8,128)S(1)}, s32[]{:T(128)}, /*index=5*/bf16[122...) while((s32[]{:T(128)}, f32[2,768]{1,0:T(2,128)S(1)}, ...), condition=%wide.region_10.11_spmd.clone, body=%wide.region_5.10_spmd.clone.sunk | while | flops 620304384 | bytes 19387720 | solution.py:104
  470.2 7.1 %conditional.3 = ((f32[2,768]{1,0:T(2,128)S(1)}, f32[2,768]{1,0:T(2,128)S(1)}, f32[768,2,128]{2,0,1:T(8,128)S(1)})) conditional(s32[]{:T(128)} %convert_element_type.76, (f32[2,768]{1,0:T(2,128)S(1)}, f32[2,768]{1,0:T(2,128)S(1)}, f32[768,2,128]{2,0,1:T(8,128)S(1)}) %tuple.106, (s32[]{:T(128)}, s32[768]{0:T(1024)S(1)}, s32[]{:T(128)}, ...), branch_computations={%region_6.6_spmd, %region_7.9_spmd} | conditional | flops 620304384 | bytes 19384402 | solution.py:101
  474.0 3.3 fusion.13
  477.4 7.1 %conditional.3 = ((f32[2,768]{1,0:T(2,128)S(1)}, f32[2,768]{1,0:T(2,128)S(1)}, f32[768,2,128]{2,0,1:T(8,128)S(1)})) conditional(s32[]{:T(128)} %convert_element_type.76, (f32[2,768]{1,0:T(2,128)S(1)}, f32[2,768]{1,0:T(2,128)S(1)}, f32[768,2,128]{2,0,1:T(8,128)S(1)}) %tuple.106, (s32[]{:T(128)}, s32[768]{0:T(1024)S(1)}, s32[]{:T(128)}, ...), branch_computations={%region_6.6_spmd, %region_7.9_spmd} | conditional | flops 620304384 | bytes 19384402 | solution.py:101
  477.8 2.1 fusion.4
  481.2 3.3 fusion.13
  484.5 7.1 %conditional.3 = ((f32[2,768]{1,0:T(2,128)S(1)}, f32[2,768]{1,0:T(2,128)S(1)}, f32[768,2,128]{2,0,1:T(8,128)S(1)})) conditional(s32[]{:T(128)} %convert_element_type.76, (f32[2,768]{1,0:T(2,128)S(1)}, f32[2,768]{1,0:T(2,128)S(1)}, f32[768,2,128]{2,0,1:T(8,128)S(1)}) %tuple.106, (s32[]{:T(128)}, s32[768]{0:T(1024)S(1)}, s32[]{:T(128)}, ...), branch_computations={%region_6.6_spmd, %region_7.9_spmd} | conditional | flops 620304384 | bytes 19384402 | solution.py:101
  484.9 2.1 fusion.4
  488.3 3.3 fusion.13
  491.6 7.1 %conditional.3 = ((f32[2,768]{1,0:T(2,128)S(1)}, f32[2,768]{1,0:T(2,128)S(1)}, f32[768,2,128]{2,0,1:T(8,128)S(1)})) conditional(s32[]{:T(128)} %convert_element_type.76, (f32[2,768]{1,0:T(2,128)S(1)}, f32[2,768]{1,0:T(2,128)S(1)}, f32[768,2,128]{2,0,1:T(8,128)S(1)}) %tuple.106, (s32[]{:T(128)}, s32[768]{0:T(1024)S(1)}, s32[]{:T(128)}, ...), branch_computations={%region_6.6_spmd, %region_7.9_spmd} | conditional | flops 620304384 | bytes 19384402 | solution.py:101
  492.1 2.1 fusion.4
  495.5 3.3 fusion.13
  498.8 7.1 %conditional.3 = ((f32[2,768]{1,0:T(2,128)S(1)}, f32[2,768]{1,0:T(2,128)S(1)}, f32[768,2,128]{2,0,1:T(8,128)S(1)})) conditional(s32[]{:T(128)} %convert_element_type.76, (f32[2,768]{1,0:T(2,128)S(1)}, f32[2,768]{1,0:T(2,128)S(1)}, f32[768,2,128]{2,0,1:T(8,128)S(1)}) %tuple.106, (s32[]{:T(128)}, s32[768]{0:T(1024)S(1)}, s32[]{:T(128)}, ...), branch_computations={%region_6.6_spmd, %region_7.9_spmd} | conditional | flops 620304384 | bytes 19384402 | solution.py:101
  499.2 2.1 fusion.4
  502.6 3.3 fusion.13
  505.9 7.1 %conditional.3 = ((f32[2,768]{1,0:T(2,128)S(1)}, f32[2,768]{1,0:T(2,128)S(1)}, f32[768,2,128]{2,0,1:T(8,128)S(1)})) conditional(s32[]{:T(128)} %convert_element_type.76, (f32[2,768]{1,0:T(2,128)S(1)}, f32[2,768]{1,0:T(2,128)S(1)}, f32[768,2,128]{2,0,1:T(8,128)S(1)}) %tuple.106, (s32[]{:T(128)}, s32[768]{0:T(1024)S(1)}, s32[]{:T(128)}, ...), branch_computations={%region_6.6_spmd, %region_7.9_spmd} | conditional | flops 620304384 | bytes 19384402 | solution.py:101
  506.4 2.1 fusion.4
  509.8 3.3 fusion.13
  513.1 7.1 %conditional.3 = ((f32[2,768]{1,0:T(2,128)S(1)}, f32[2,768]{1,0:T(2,128)S(1)}, f32[768,2,128]{2,0,1:T(8,128)S(1)})) conditional(s32[]{:T(128)} %convert_element_type.76, (f32[2,768]{1,0:T(2,128)S(1)}, f32[2,768]{1,0:T(2,128)S(1)}, f32[768,2,128]{2,0,1:T(8,128)S(1)}) %tuple.106, (s32[]{:T(128)}, s32[768]{0:T(1024)S(1)}, s32[]{:T(128)}, ...), branch_computations={%region_6.6_spmd, %region_7.9_spmd} | conditional | flops 620304384 | bytes 19384402 | solution.py:101
  513.5 2.1 fusion.4
  516.9 3.3 fusion.13
  520.2 7.1 %conditional.3 = ((f32[2,768]{1,0:T(2,128)S(1)}, f32[2,768]{1,0:T(2,128)S(1)}, f32[768,2,128]{2,0,1:T(8,128)S(1)})) conditional(s32[]{:T(128)} %convert_element_type.76, (f32[2,768]{1,0:T(2,128)S(1)}, f32[2,768]{1,0:T(2,128)S(1)}, f32[768,2,128]{2,0,1:T(8,128)S(1)}) %tuple.106, (s32[]{:T(128)}, s32[768]{0:T(1024)S(1)}, s32[]{:T(128)}, ...), branch_computations={%region_6.6_spmd, %region_7.9_spmd} | conditional | flops 620304384 | bytes 19384402 | solution.py:101
  520.7 2.1 fusion.4
  524.1 3.3 fusion.13
  527.4 7.1 %conditional.3 = ((f32[2,768]{1,0:T(2,128)S(1)}, f32[2,768]{1,0:T(2,128)S(1)}, f32[768,2,128]{2,0,1:T(8,128)S(1)})) conditional(s32[]{:T(128)} %convert_element_type.76, (f32[2,768]{1,0:T(2,128)S(1)}, f32[2,768]{1,0:T(2,128)S(1)}, f32[768,2,128]{2,0,1:T(8,128)S(1)}) %tuple.106, (s32[]{:T(128)}, s32[768]{0:T(1024)S(1)}, s32[]{:T(128)}, ...), branch_computations={%region_6.6_spmd, %region_7.9_spmd} | conditional | flops 620304384 | bytes 19384402 | solution.py:101
  527.8 2.1 fusion.4
  531.2 3.3 fusion.13
  534.5 7.1 %conditional.3 = ((f32[2,768]{1,0:T(2,128)S(1)}, f32[2,768]{1,0:T(2,128)S(1)}, f32[768,2,128]{2,0,1:T(8,128)S(1)})) conditional(s32[]{:T(128)} %convert_element_type.76, (f32[2,768]{1,0:T(2,128)S(1)}, f32[2,768]{1,0:T(2,128)S(1)}, f32[768,2,128]{2,0,1:T(8,128)S(1)}) %tuple.106, (s32[]{:T(128)}, s32[768]{0:T(1024)S(1)}, s32[]{:T(128)}, ...), branch_computations={%region_6.6_spmd, %region_7.9_spmd} | conditional | flops 620304384 | bytes 19384402 | solution.py:101
  535.0 2.1 fusion.4
  538.4 3.3 fusion.13
  541.7 7.1 %conditional.3 = ((f32[2,768]{1,0:T(2,128)S(1)}, f32[2,768]{1,0:T(2,128)S(1)}, f32[768,2,128]{2,0,1:T(8,128)S(1)})) conditional(s32[]{:T(128)} %convert_element_type.76, (f32[2,768]{1,0:T(2,128)S(1)}, f32[2,768]{1,0:T(2,128)S(1)}, f32[768,2,128]{2,0,1:T(8,128)S(1)}) %tuple.106, (s32[]{:T(128)}, s32[768]{0:T(1024)S(1)}, s32[]{:T(128)}, ...), branch_computations={%region_6.6_spmd, %region_7.9_spmd} | conditional | flops 620304384 | bytes 19384402 | solution.py:101
  542.1 2.1 fusion.4
  545.5 3.3 fusion.13
  548.8 7.1 %conditional.3 = ((f32[2,768]{1,0:T(2,128)S(1)}, f32[2,768]{1,0:T(2,128)S(1)}, f32[768,2,128]{2,0,1:T(8,128)S(1)})) conditional(s32[]{:T(128)} %convert_element_type.76, (f32[2,768]{1,0:T(2,128)S(1)}, f32[2,768]{1,0:T(2,128)S(1)}, f32[768,2,128]{2,0,1:T(8,128)S(1)}) %tuple.106, (s32[]{:T(128)}, s32[768]{0:T(1024)S(1)}, s32[]{:T(128)}, ...), branch_computations={%region_6.6_spmd, %region_7.9_spmd} | conditional | flops 620304384 | bytes 19384402 | solution.py:101
  549.3 2.1 fusion.4
  552.7 3.3 fusion.13
  556.0 7.1 %conditional.3 = ((f32[2,768]{1,0:T(2,128)S(1)}, f32[2,768]{1,0:T(2,128)S(1)}, f32[768,2,128]{2,0,1:T(8,128)S(1)})) conditional(s32[]{:T(128)} %convert_element_type.76, (f32[2,768]{1,0:T(2,128)S(1)}, f32[2,768]{1,0:T(2,128)S(1)}, f32[768,2,128]{2,0,1:T(8,128)S(1)}) %tuple.106, (s32[]{:T(128)}, s32[768]{0:T(1024)S(1)}, s32[]{:T(128)}, ...), branch_computations={%region_6.6_spmd, %region_7.9_spmd} | conditional | flops 620304384 | bytes 19384402 | solution.py:101
  556.4 2.1 fusion.4
  559.8 3.3 fusion.13
  563.1 7.1 %conditional.3 = ((f32[2,768]{1,0:T(2,128)S(1)}, f32[2,768]{1,0:T(2,128)S(1)}, f32[768,2,128]{2,0,1:T(8,128)S(1)})) conditional(s32[]{:T(128)} %convert_element_type.76, (f32[2,768]{1,0:T(2,128)S(1)}, f32[2,768]{1,0:T(2,128)S(1)}, f32[768,2,128]{2,0,1:T(8,128)S(1)}) %tuple.106, (s32[]{:T(128)}, s32[768]{0:T(1024)S(1)}, s32[]{:T(128)}, ...), branch_computations={%region_6.6_spmd, %region_7.9_spmd} | conditional | flops 620304384 | bytes 19384402 | solution.py:101
  563.6 2.1 fusion.4
  567.0 3.3 fusion.13
  570.3 7.1 %conditional.3 = ((f32[2,768]{1,0:T(2,128)S(1)}, f32[2,768]{1,0:T(2,128)S(1)}, f32[768,2,128]{2,0,1:T(8,128)S(1)})) conditional(s32[]{:T(128)} %convert_element_type.76, (f32[2,768]{1,0:T(2,128)S(1)}, f32[2,768]{1,0:T(2,128)S(1)}, f32[768,2,128]{2,0,1:T(8,128)S(1)}) %tuple.106, (s32[]{:T(128)}, s32[768]{0:T(1024)S(1)}, s32[]{:T(128)}, ...), branch_computations={%region_6.6_spmd, %region_7.9_spmd} | conditional | flops 620304384 | bytes 19384402 | solution.py:101
  570.7 2.1 fusion.4
  574.1 3.3 fusion.13
  577.4 7.1 %conditional.3 = ((f32[2,768]{1,0:T(2,128)S(1)}, f32[2,768]{1,0:T(2,128)S(1)}, f32[768,2,128]{2,0,1:T(8,128)S(1)})) conditional(s32[]{:T(128)} %convert_element_type.76, (f32[2,768]{1,0:T(2,128)S(1)}, f32[2,768]{1,0:T(2,128)S(1)}, f32[768,2,128]{2,0,1:T(8,128)S(1)}) %tuple.106, (s32[]{:T(128)}, s32[768]{0:T(1024)S(1)}, s32[]{:T(128)}, ...), branch_computations={%region_6.6_spmd, %region_7.9_spmd} | conditional | flops 620304384 | bytes 19384402 | solution.py:101
  577.9 2.1 fusion.4
  581.3 3.3 fusion.13
  (223 shorter events, 70.5 us)
Async XLA Ops:
  7.2 10.9 %copy-start.6 = (s32[16384]{0:T(1024)S(1)}, s32[16384]{0:T(1024)}, u32[]{:S(2)}) copy-start(s32[16384]{0:T(1024)} %constant.135) | copy-start | bytes 196612
  7.2 8.2 %copy-start.9 = (f32[3,3,256]{2,1,0:T(4,128)S(1)}, f32[3,3,256]{2,1,0:T(4,128)}, u32[]{:S(2)}) copy-start(f32[3,3,256]{2,1,0:T(4,128)} %param.20) | copy-start | bytes 27652
  7.2 8.2 %copy-start.7 = (f32[256,16]{0,1:T(8,128)S(1)}, f32[256,16]{0,1:T(8,128)}, u32[]{:S(2)}) copy-start(f32[256,16]{0,1:T(8,128)} %param.21) | copy-start | bytes 49156
  7.2 8.1 %copy-start.8 = (f32[256,16]{0,1:T(8,128)S(1)}, f32[256,16]{0,1:T(8,128)}, u32[]{:S(2)}) copy-start(f32[256,16]{0,1:T(8,128)} %param.22) | copy-start | bytes 49156
  7.2 302.8 %all-gather.6.cloned.1.call-start = ((), (), s32[]{:S(2)}) async-start(), calls=%async_computation | async-start | bytes 6684672 | tf_op jit(solution)/shard_map/all_gather | solution.py:170
  8.0 110.8 %collective-permute-start = (s32[2]{0:T(128)S(1)}, s32[2]{0:T(128)S(1)}, u32[]{:S(2)}, u32[]{:S(2)}) collective-permute-start(s32[2]{0:T(128)S(1)} %slice.41), channel_id=1, source_target_pairs={{0,16},{16,32},{32,48},{48,64},{64,80},{80,96},{96,112},{112,128},... | collective-permute-start | bytes 32 | tf_op jit(solution)/shard_map/ppermute | solution.py:20
  15.5 2.4 copy-start.4
  15.6 0.6 copy-start.2
  119.1 6.4 %copy-start.11 = (f32[128]{0:T(128)S(1)}, f32[128]{0:T(128)}, u32[]{:S(2)}) copy-start(f32[128]{0:T(128)} %iota_subtract_fusion) | copy-start | bytes 1540
  177.3 28.7 %copy-start.1 = (f32[6,256,16]{2,0,1:T(8,128)S(1)}, f32[6,256,16]{2,0,1:T(8,128)}, u32[]{:S(2)}) copy-start(f32[6,256,16]{2,0,1:T(8,128)} %copy.38) | copy-start | bytes 294916
  177.3 28.7 %copy-start.3 = (f32[256,16]{1,0:T(8,128)S(1)}, f32[256,16]{1,0:T(8,128)}, u32[]{:S(2)}) copy-start(f32[256,16]{1,0:T(8,128)} %copy-done.2) | copy-start | bytes 49156
  177.3 28.7 %copy-start.5 = (f32[256,16]{1,0:T(8,128)S(1)}, f32[256,16]{1,0:T(8,128)}, u32[]{:S(2)}) copy-start(f32[256,16]{1,0:T(8,128)} %copy-done.4) | copy-start | bytes 49156
  177.3 28.7 %copy-start.12 = (f32[128]{0:T(128)S(1)}, f32[128]{0:T(128)}, u32[]{:S(2)}) copy-start(f32[128]{0:T(128)} %iota_add_fusion) | copy-start | bytes 1540
  206.1 5.2 copy-start.10
  212.3 187.3 %all-gather.8.cloned.1.call-start = ((), (), s32[]{:S(2)}) async-start(), calls=%async_computation.1 | async-start | bytes 6684672 | tf_op jit(solution)/shard_map/all_gather | solution.py:187
  310.0 4.6 copy-start
  323.2 146.9 %all-gather.10.cloned.1.call-start = ((), (), s32[]{:S(2)}) async-start(), calls=%async_computation.2 | async-start | bytes 6684672 | tf_op jit(solution)/shard_map/all_gather | solution.py:188
Sparse Core Ops, SparseCore 0:
  212.4 97.5 all-gather.5
  323.3 76.1 all-gather.7
  402.3 67.7 all-gather.9
where the time goes:
time: 594 us; the launch traced here: 592 us
  waiting for transfers between devices  243 us (41%)
  matrix products  134 us (23%)
  local copies, waits for them, and re-layouts  108 us (18%)
  other arithmetic  46.3 us (8%)
  blocking collectives  42.4 us (7%)
  between operations  14 us (2%)
    all_gather x1, waiting for transfers between devices, per_device(): portion = lax.all_gather(hyena_out, 'mp', axis=1, tiled=True)  97.7 us
    gather x2, local copies, waits for them, and re-layouts, per_device(): kernel[:, np.maximum(lag_index, 0)]  80.1 us
    all_gather x1, waiting for transfers between devices, per_device(): lax.all_gather(key_rows, 'ctx', axis=0, tiled=True)  74.8 us
    all_gather x1, waiting for transfers between devices, per_device(): lax.all_gather(value_rows, 'ctx', axis=0, tiled=True)  70.6 us
    dot_general x16, matrix products, attend(): jnp.einsum('hqk,khd->qhd', weights.astype(jnp.bfloat16), value_rows, pref...  52.3 us
    all_gather x2, blocking collectives, entering(): gathered = jax.tree.map(lambda a: lax.all_gather(a, axis), part)  42.4 us
    dot_general x16, matrix products, attend(): jnp.einsum('qhd,khd->hqk', queries, key_rows, preferred_element_type=jnp....  33.1 us
    dot_general x1, matrix products, per_device(): jnp.einsum('cts,bsc->btc', toeplitz, gate_blocks, precision=lax.Precision...  28.7 us
  transfers between devices with their start and end apart: 4, of which 3 were waited for; matrix products, arithmetic and copies ran while one was open for 15% of the time, Pallas kernels for 0%

commit v1 on v0

v1 whole, which is shorter than its diff:
```python
import functools
import math

import jax
import jax.numpy as jnp
from jax import lax
from jax.experimental import pallas as pl
from jax.experimental.pallas import tpu as pltpu
from jax.sharding import PartitionSpec as P

MESH = pl.DeviceIdType.MESH
HEAD_DIM = 128
TAPS = 3
SEGS = 8
NEG_FILL = -1e30
NORM_EPSILON = 1e-06

CTX = 16
MP = 16
PLANE = 8
CHUNKS = 4
Q_TILE = 256


def mixer_kernel(
    ids_ref, table_hbm, filt_ref, rates_ref, resid_ref, skip_ref, w_hbm,
    hyena_hbm, att_hbm,
    table, w, feats, gate, lead, rim, decay, weight, ends, starts, states,
    x, kv, qs, kv_out, q_out, q_acc, q_max, att,
    local_sem, rim_sem, state_send, state_recv,
    y_send, y_recv, z_send, z_recv,
    h_send, h_recv, c_send, c_recv, r_send, r_recv, o_sem,
):
    rows = feats.shape[1] - 8
    chans = feats.shape[2]
    modes = decay.shape[0]
    steps = rows // SEGS
    part = rows // CHUNKS
    half = part // 2
    all_chans = x.shape[1]
    total_len = CTX * rows

    me = lax.axis_index("ctx")
    mp = lax.axis_index("mp")
    core = me % 2
    xpos = (me // 2) % 4
    yhi = me // 8
    zpos = mp % PLANE
    ylo = mp // PLANE
    sibling = me + 1 - 2 * core
    opposite = (me + 8) % CTX
    x_right = yhi * 8 + 2 * ((xpos + 1) % 4) + core
    x_left = yhi * 8 + 2 * ((xpos + 3) % 4) + core
    x_far = yhi * 8 + 2 * ((xpos + 2) % 4) + core
    z_right = ylo * PLANE + (zpos + 1) % PLANE
    z_left = ylo * PLANE + (zpos + PLANE - 1) % PLANE
    y_other = (1 - ylo) * PLANE + zpos

    def to_ctx(src, dst, send, recv, target):
        return pltpu.make_async_remote_copy(
            src_ref=src, dst_ref=dst, send_sem=send, recv_sem=recv,
            device_id={"ctx": target}, device_id_type=MESH,
        )

    def to_mp(src, dst, send, recv, target):
        return pltpu.make_async_remote_copy(
            src_ref=src, dst_ref=dst, send_sem=send, recv_sem=recv,
            device_id={"mp": target}, device_id_type=MESH,
        )

    table_copy = pltpu.make_async_copy(table_hbm, table, local_sem.at[0])
    table_copy.start()
    w_copy = pltpu.make_async_copy(w_hbm, w, local_sem.at[1])
    w_copy.start()

    barrier = pltpu.get_barrier_semaphore()
    for k in range(1, CTX):
        pl.semaphore_signal(
            barrier, inc=1, device_id={"ctx": (me + k) % CTX}, device_id_type=MESH
        )
    for other in (z_right, z_left, y_other):
        pl.semaphore_signal(barrier, inc=1, device_id={"mp": other}, device_id_type=MESH)
    pl.semaphore_wait(barrier, CTX - 1 + 3)

    rim_copy = to_ctx(
        ids_ref.at[:, pl.ds(rows - 128, 128)], rim, rim_sem.at[0], rim_sem.at[1], (me + 1) % CTX
    )
    rim_copy.start()

    vocab = table.shape[1]

    def looked(ids, feature):
        at = lax.broadcasted_iota(jnp.int32, (vocab, ids.shape[1]), 0)
        hot = (at == ids).astype(jnp.float32).astype(jnp.bfloat16)
        return lax.dot_general(
            hot, table[feature], (((0,), (0,)), ((), ())), preferred_element_type=jnp.float32
        )

    damping = rates_ref[...] / total_len
    twice = 2.0 * damping
    small = twice * (
        1.0
        - twice
        * (
            0.5
            - twice
            * (1.0 / 6 - twice * (1.0 / 24 - twice * (1.0 / 120 - twice * (1.0 / 720))))
        )
    )
    grown = jnp.where(twice < 0.1, small, 1.0 - jnp.exp(-twice))
    mode_weight = resid_ref[...] * jnp.sqrt(grown)
    one_step = jnp.exp(-damping)
    for r in range(modes):
        decay[r] = jnp.broadcast_to(one_step[r : r + 1, :], (SEGS, chans))
        weight[r] = jnp.broadcast_to(mode_weight[r : r + 1, :], (SEGS, chans))

    table_copy.wait()
    for j in range(3):
        feats[j, 8:, :] = looked(ids_ref[...], j)
    rim_copy.wait_recv()
    for j in range(3):
        before = looked(rim[...], j)[120:128, :]
        feats[j, 0:8, :] = jnp.where(me > 0, before, 0.0)

    def smooth(j, at, count):
        total = filt_ref[0, j : j + 1, :] * feats[j, 8 + at : 8 + at + count, :]
        for tap in range(1, TAPS):
            total = total + filt_ref[tap, j : j + 1, :] * feats[
                j, 8 + at - tap : 8 + at - tap + count, :
            ]
        return total

    groups = [(g, slice(g * 128, (g + 1) * 128)) for g in range(chans // 128)]
    for at in range(0, rows, 96):
        gated = smooth(1, at, 96) * smooth(2, at, 96)
        led = smooth(0, at, 96)
        for g, lanes in groups:
            gate[g, at : at + 96, :] = gated[:, lanes]
            lead[g, at : at + 96, :] = led[:, lanes]

    for g, lanes in groups:
        fade = decay[:, :, lanes]

        def ended(i, state, g=g, fade=fade):
            row = gate[g, pl.ds(i, SEGS, stride=steps), :]
            return fade * state + row[None]

        ends[:, :, lanes] = lax.fori_loop(
            0, steps, ended, jnp.zeros((modes, SEGS, 128), jnp.float32)
        )
    segment_fade = jnp.exp(-damping * steps)
    running = jnp.zeros((modes, chans), jnp.float32)
    for j in range(SEGS):
        starts[:, j, :] = running
        running = segment_fade * running + ends[:, j, :]
    states[me] = running
    state_copies = []
    for k in range(1, CTX):
        copy = to_ctx(
            states.at[me], states.at[me], state_send.at[k - 1], state_recv.at[k - 1],
            (me + k) % CTX,
        )
        copy.start()
        state_copies.append(copy)
    for k in range(1, CTX):
        source = (me + CTX - k) % CTX
        to_ctx(
            states.at[source], states.at[source], state_send.at[k - 1], state_recv.at[k - 1],
            (me + k) % CTX,
        ).wait_recv()

    def gathered(k, total):
        gap = jnp.maximum(me - 1 - k, 0).astype(jnp.float32) * rows
        return total + jnp.where(k < me, jnp.exp(-damping * gap) * states[k], 0.0)

    incoming = lax.fori_loop(0, CTX, gathered, jnp.zeros((modes, chans), jnp.float32))
    for j in range(SEGS):
        starts[:, j, :] += jnp.exp(-damping * (steps * j)) * incoming

    for g, lanes in groups:
        fade = decay[:, :, lanes]
        skip = skip_ref[:, lanes]

        def stepped(i, state, g=g, lanes=lanes, fade=fade, skip=skip):
            at = pl.ds(i, SEGS, stride=steps)
            row = gate[g, at, :]
            state = fade * state + row[None]
            conv = jnp.sum(weight[:, :, lanes] * state, axis=0)
            gate[g, at, :] = lead[g, at, :] * (conv + skip * row)
            return state

        lax.fori_loop(0, steps, stepped, starts[:, :, lanes])

    def columns(ylo_at, z_at):
        return pl.ds(pl.multiple_of((ylo_at * PLANE + z_at) * chans, chans), chans)

    mine = columns(ylo, zpos)
    x[:, mine] = jnp.concatenate([gate[g] for g, _ in groups], axis=1).astype(jnp.bfloat16)
    hyena_copy = pltpu.make_async_copy(x.at[:, mine], hyena_hbm, local_sem.at[2])
    hyena_copy.start()

    def z_copy(n, plane, step, direction):
        away = step - 1
        origin = (zpos + PLANE - away) % PLANE if direction == 0 else (zpos + away) % PLANE
        target = z_right if direction == 0 else z_left
        count, shift = (half, direction * half) if step == 4 else (part, 0)
        at = pl.ds(pl.multiple_of(n * part + shift, 16), count)
        ref = x.at[at, columns(ylo if plane == 0 else 1 - ylo, origin)]
        k = ((n * 2 + plane) * 4 + step - 1) * 2 + direction
        return to_mp(ref, ref, z_send.at[k], z_recv.at[k], target)

    def z_wait(n, plane, step, direction):
        origin = (zpos + PLANE - step) % PLANE if direction == 0 else (zpos + step) % PLANE
        target = z_right if direction == 0 else z_left
        count, shift = (half, direction * half) if step == 4 else (part, 0)
        at = pl.ds(pl.multiple_of(n * part + shift, 16), count)
        ref = x.at[at, columns(ylo if plane == 0 else 1 - ylo, origin)]
        k = ((n * 2 + plane) * 4 + step - 1) * 2 + direction
        to_mp(ref, ref, z_send.at[k], z_recv.at[k], target).wait_recv()

    def y_copy(n, ylo_at):
        ref = x.at[pl.ds(pl.multiple_of(n * part, 16), part), columns(ylo_at, zpos)]
        return to_mp(ref, ref, y_send.at[n], y_recv.at[n], y_other)

    def begin(n):
        y_copy(n, ylo).start()
        for direction in (0, 1):
            z_copy(n, 0, 1, direction).start()

    def kv_rows(owner, n, shift=0, count=part):
        return kv.at[pl.ds(pl.multiple_of(owner * rows + n * part + shift, 16), count), :]

    def q_rows(which, n):
        return qs.at[which, pl.ds(pl.multiple_of(n * part, 16), part), :]

    def out_copies(n):
        at = pl.ds(pl.multiple_of(n * part, 16), part)
        return (
            to_ctx(kv_out.at[at, :], kv_rows(me, n), h_send.at[n * 2], h_recv.at[n * 2], opposite),
            to_ctx(
                q_out.at[at, :], q_rows(0, n), h_send.at[n * 2 + 1], h_recv.at[n * 2 + 1], opposite
            ),
        )

    def out_waits(n):
        at = pl.ds(pl.multiple_of(n * part, 16), part)
        to_ctx(
            kv_out.at[at, :], kv_rows(opposite, n), h_send.at[n * 2], h_recv.at[n * 2], opposite
        ).wait_recv()
        to_ctx(
            q_out.at[at, :], q_rows(0, n), h_send.at[n * 2 + 1], h_recv.at[n * 2 + 1], opposite
        ).wait_recv()

    def across(owner):
        return (owner + 8) % CTX

    def ring_part(n, which, step, direction, outgoing):
        if step == 1:
            owner = me if outgoing else (x_left if direction == 0 else x_right)
            shift, count = 0, part
        else:
            near = x_left if direction == 0 else x_right
            owner = near if outgoing else x_far
            shift, count = direction * half, half
        if which == 1:
            owner = across(owner)
        ref = kv_rows(owner, n, shift, count)
        k = ((n * 2 + which) * 2 + step - 1) * 2 + direction
        target = x_right if direction == 0 else x_left
        return ref, to_ctx(ref, ref, r_send.at[k], r_recv.at[k], target)

    def core_part(n, kind, outgoing):
        if kind < 2:
            owner = me if outgoing else sibling
            if kind == 1:
                owner = across(owner)
            ref = kv_rows(owner, n)
        else:
            which, step, direction = (kind - 2) // 4, (kind - 2) // 2 % 2 + 1, (kind - 2) % 2
            near = x_left if direction == 0 else x_right
            owner = near if step == 1 else x_far
            if not outgoing:
                owner = owner + 1 - 2 * core
            if which == 1:
                owner = across(owner)
            ref = kv_rows(owner, n, *((0, part) if step == 1 else (direction * half, half)))
        k = n * 10 + kind
        return to_ctx(ref, ref, c_send.at[k], c_recv.at[k], sibling)

    def spread(n, which):
        core_part(n, which, True).start()
        for direction in (0, 1):
            ring_part(n, which, 1, direction, True)[1].start()

    def ring_tick(n, step):
        for which in (0, 1):
            for direction in (0, 1):
                ring_part(n, which, step, direction, False)[1].wait_recv()
                if step == 1:
                    ring_part(n, which, 2, direction, True)[1].start()
                core_part(n, 2 + which * 4 + (step - 1) * 2 + direction, True).start()

    own_head = yhi

    def project(n):
        at = pl.ds(pl.multiple_of(n * part, 16), part)
        wide = x[at, :].astype(jnp.float32)
        squares = jnp.sum(wide * wide, axis=1, keepdims=True)
        norm = lax.rsqrt(squares / all_chans + NORM_EPSILON)
        kv_at = pl.ds(pl.multiple_of(me * rows + n * part, 16), part)
        for j in range(3):
            scale = norm * (math.log2(math.e) / math.sqrt(HEAD_DIM)) if j == 0 else norm
            made = jnp.dot(x[at, :], w[j], preferred_element_type=jnp.float32) * scale
            made = made.astype(jnp.bfloat16)
            first, second = made[:, :HEAD_DIM], made[:, HEAD_DIM:]
            kept = jnp.where(own_head == 0, first, second)
            sent = jnp.where(own_head == 0, second, first)
            if j == 0:
                qs[1, at, :] = kept
                q_out[at, :] = sent
            else:
                lanes = slice((j - 1) * HEAD_DIM, j * HEAD_DIM)
                kv[kv_at, lanes] = kept
                kv_out[at, lanes] = sent

    begin(0)
    w_copy.wait()

    def one_chunk(n, carry):
        live, late = n < CHUNKS, n > 0

        @pl.when(live)
        def _():
            y_copy(n, 1 - ylo).wait_recv()
            for direction in (0, 1):
                z_copy(n, 1, 1, direction).start()

        for step in (1, 2, 3):

            @pl.when(live)
            def _(step=step):
                for plane in (0, 1):
                    for direction in (0, 1):
                        z_wait(n, plane, step, direction)
                        z_copy(n, plane, step + 1, direction).start()

            if step == 2:

                @pl.when(n + 1 < CHUNKS)
                def _():
                    begin(n + 1)

            @pl.when(late)
            def _(step=step):
                if step == 1:
                    out_waits(n - 1)
                    spread(n - 1, 1)
                else:
                    ring_tick(n - 1, step - 1)

        @pl.when(live)
        def _():
            for plane in (0, 1):
                for direction in (0, 1):
                    z_wait(n, plane, 4, direction)
            project(n)
            for copy in out_copies(n):
                copy.start()
            spread(n, 0)

        return carry

    lax.fori_loop(0, CHUNKS + 1, one_chunk, 0)

    def core_arrived(n, carry):
        for kind in range(10):
            core_part(n, kind, False).wait_recv()
        return carry

    lax.fori_loop(0, CHUNKS, core_arrived, 0)

    ones = jnp.ones((rows, HEAD_DIM), jnp.bfloat16)

    def attend(queries, key_at, shift):
        block = kv[pl.ds(pl.multiple_of(key_at, 16), rows), :]
        scores = lax.dot_general(
            queries, block[:, :HEAD_DIM], (((1,), (1,)), ((), ())),
            preferred_element_type=jnp.float32,
        )
        if shift is not None:
            row = lax.broadcasted_iota(jnp.int32, scores.shape, 0) + shift
            col = lax.broadcasted_iota(jnp.int32, scores.shape, 1)
            scores = jnp.where(col <= row, scores, NEG_FILL)
        old = q_max[...]
        new = jnp.maximum(old, jnp.max(scores, axis=1, keepdims=True))
        wide = jnp.concatenate([new] * (rows // 128), axis=1)
        weights = jnp.exp2(scores - wide).astype(jnp.bfloat16)
        values = jnp.concatenate([block[:, HEAD_DIM:], ones], axis=1)
        shrink = jnp.exp2(old - new)
        q_acc[...] = q_acc[...] * jnp.concatenate([shrink, shrink], axis=1) + jnp.dot(
            weights, values, preferred_element_type=jnp.float32
        )
        q_max[...] = new

    head_lanes = pl.ds(pl.multiple_of(own_head * HEAD_DIM, HEAD_DIM), HEAD_DIM)
    other_lanes = pl.ds(pl.multiple_of((1 - own_head) * HEAD_DIM, HEAD_DIM), HEAD_DIM)

    def attend_set(which, owner):
        for tile in range(rows // Q_TILE):
            at = slice(tile * Q_TILE, (tile + 1) * Q_TILE)
            q_acc[...] = jnp.zeros_like(q_acc)
            q_max[...] = jnp.full_like(q_max, NEG_FILL)

            def one_block(k, carry, at=at):
                attend(qs[which, at, :], k * rows, None)
                return carry

            lax.fori_loop(0, owner, one_block, 0)
            attend(qs[which, at, :], owner * rows, tile * Q_TILE)
            done = (q_acc[:, :HEAD_DIM] / q_acc[:, HEAD_DIM:]).astype(jnp.bfloat16)
            if which == 0:
                q_out[at, :] = done
            else:
                att[at, head_lanes] = done

    for n in range(CHUNKS):
        for copy in out_copies(n):
            copy.wait_send()
    attend_set(0, opposite)
    back = to_ctx(q_out, att.at[:, head_lanes], o_sem.at[0], o_sem.at[1], opposite)
    back.start()
    attend_set(1, me)
    to_ctx(q_out, att.at[:, other_lanes], o_sem.at[0], o_sem.at[1], opposite).wait_recv()
    att_copy = pltpu.make_async_copy(att, att_hbm, local_sem.at[3])
    att_copy.start()

    rim_copy.wait_send()
    for copy in state_copies:
        copy.wait_send()
    back.wait_send()

    def sent(n, carry):
        y_copy(n, ylo).wait_send()
        for direction in (0, 1):
            for plane in (0, 1):
                for step in (1, 2, 3, 4):
                    z_copy(n, plane, step, direction).wait_send()
            for which in (0, 1):
                for step in (1, 2):
                    ring_part(n, which, step, direction, True)[1].wait_send()
        for kind in range(10):
            core_part(n, kind, True).wait_send()
        return carry

    lax.fori_loop(0, CHUNKS, sent, 0)
    hyena_copy.wait()
    att_copy.wait()


def per_device(token_ids, feature_table, short_filter, rates, residues, skip_weight, w_qkv):
    rows = token_ids.shape[0]
    vocab, _, chans = feature_table.shape
    modes = rates.shape[1]
    all_chans, _, width = w_qkv.shape
    f32, bf16 = jnp.float32, jnp.bfloat16
    dma = pltpu.SemaphoreType.DMA
    vmem = pl.BlockSpec(memory_space=pltpu.VMEM)
    hbm = pl.BlockSpec(memory_space=pl.ANY)
    return pl.pallas_call(
        mixer_kernel,
        out_shape=(
            jax.ShapeDtypeStruct((rows, chans), bf16),
            jax.ShapeDtypeStruct((rows, width), bf16),
        ),
        in_specs=[vmem, hbm, vmem, vmem, vmem, vmem, hbm],
        out_specs=(hbm, hbm),
        scratch_shapes=[
            pltpu.VMEM((3, vocab, chans), bf16),
            pltpu.VMEM((3, all_chans, width), bf16),
            pltpu.VMEM((3, 8 + rows, chans), f32),
            pltpu.VMEM((chans // 128, rows, 128), f32),
            pltpu.VMEM((chans // 128, rows, 128), f32),
            pltpu.VMEM((1, 128), jnp.int32),
            pltpu.VMEM((modes, SEGS, chans), f32),
            pltpu.VMEM((modes, SEGS, chans), f32),
            pltpu.VMEM((modes, SEGS, chans), f32),
            pltpu.VMEM((modes, SEGS, chans), f32),
            pltpu.VMEM((CTX, modes, chans), f32),
            pltpu.VMEM((rows, all_chans), bf16),
            pltpu.VMEM((CTX * rows, 2 * HEAD_DIM), bf16),
            pltpu.VMEM((2, rows, HEAD_DIM), bf16),
            pltpu.VMEM((rows, 2 * HEAD_DIM), bf16),
            pltpu.VMEM((rows, HEAD_DIM), bf16),
            pltpu.VMEM((Q_TILE, 2 * HEAD_DIM), f32),
            pltpu.VMEM((Q_TILE, HEAD_DIM), f32),
            pltpu.VMEM((rows, width), bf16),
            dma((4,)),
            dma((2,)),
            dma((CTX - 1,)),
            dma((CTX - 1,)),
            dma((CHUNKS,)),
            dma((CHUNKS,)),
            dma((CHUNKS * 16,)),
            dma((CHUNKS * 16,)),
            dma((CHUNKS * 2,)),
            dma((CHUNKS * 2,)),
            dma((CHUNKS * 10,)),
            dma((CHUNKS * 10,)),
            dma((CHUNKS * 8,)),
            dma((CHUNKS * 8,)),
            dma((2,)),
        ],
        compiler_params=pltpu.CompilerParams(
            collective_id=0, has_side_effects=True, vmem_limit_bytes=56 * 1024 * 1024
        ),
        name="mixer",
    )(
        token_ids.reshape(1, rows),
        jnp.transpose(feature_table, (1, 0, 2)),
        short_filter,
        rates.T,
        residues.T,
        skip_weight.reshape(1, chans),
        jnp.transpose(w_qkv, (1, 0, 2)),
    )


def solution(mesh):
    in_specs = (
        P("ctx"),
        P(None, None, "mp"),
        P(None, None, "mp"),
        P("mp", None),
        P("mp", None),
        P("mp"),
        P(None, None, "mp"),
    )
    out_specs = (P("ctx", "mp"), P("ctx", "mp"))
    return jax.shard_map(
        per_device, mesh=mesh, in_specs=in_specs, out_specs=out_specs, check_vma=False
    )
```

time: 594 us -> 181 us (0.30)
  the two profiles are of different devices: /device:TPU:31 before, /device:TPU:7 now
where the time goes in v1:
time: 181 us
  Pallas kernels  176 us (97%)
  local copies, waits for them, and re-layouts  4.8 us (3%)
    pallas_call x1, Pallas kernels, per_device(): pl.pallas_call(mixer_kernel, out_shape=(jax.ShapeDtypeStruct((rows, chans...  176 us

profile of v1, /device:TPU:7, one launch (start us, length us, event | category | flops | bytes accessed | tf_op | source)
XLA Modules:
  0.0 181.2 jit_solution(72123974500120662)
XLA Ops:
  0.6 1.3 reshape.10.ids_ref
  1.9 175.8 %mixer.1 = (bf16[768,256]{1,0:T(8,128)(2,1)}, bf16[768,256]{1,0:T(8,128)(2,1)}) custom-call(s32[1,768]{1,0:T(1,128)} %reshape.10.ids_ref, bf16[3,512,256]{2,1,0:T(8,128)(2,1)} %bitcast.6, f32[3,3,256]{2,1,0:T(4,128)} %filt_ref.1, f32[16,256]{1,0:T(8,128)} %bitcast.7, f32[16,256]{1,0:T(8,128)} %bitcast.8, f32[1,256]{1,0:T(1,128)} %bitcast.9, ...), custom_call_target="tpu_custom_call" | custom-call | tf_op jit(solution)/shard_map/mixer/pallas_call | solution.py:469
  177.7 1.8 copy.11
  179.4 1.8 copy.12

commit v2 on v1

v2 whole, which is shorter than its diff:
```python
import functools
import math

import jax
import jax.numpy as jnp
from jax import lax
from jax.experimental import pallas as pl
from jax.experimental.pallas import tpu as pltpu
from jax.sharding import PartitionSpec as P

MESH = pl.DeviceIdType.MESH
HEAD_DIM = 128
TAPS = 3
SEGS = 8
NEG_FILL = -1e30
NORM_EPSILON = 1e-06

CTX = 16
MP = 16
PLANE = 8
CHUNKS = 4


def mixer_kernel(
    ids_ref, table_hbm, filt_ref, rates_ref, resid_ref, skip_ref, w_hbm,
    hyena_hbm, att_hbm,
    table, w, feats, gate, lead, rim, decay, weight, ends, starts, states,
    own, x, kv, qs, kv_out, q_out, q_acc, q_max, o_out, att,
    local_sem, rim_sem, state_send, state_recv,
    wy_send, wy_recv, wx_send, wx_recv,
    y_send, y_recv, z_send, z_recv, d_send, d_recv,
    h_send, h_recv, l_sem, c_send, c_recv, r_send, r_recv, o_send, o_recv,
):
    rows = feats.shape[1] - 8
    chans = feats.shape[2]
    modes = decay.shape[0]
    steps = rows // SEGS
    part = rows // CHUNKS
    half = part // 2
    all_chans = x.shape[1]
    total_len = CTX * rows
    span = CTX * part

    me = lax.axis_index("ctx")
    mp = lax.axis_index("mp")
    core = me % 2
    xpos = (me // 2) % 4
    yhi = me // 8
    zpos = mp % PLANE
    ylo = mp // PLANE
    sibling = me + 1 - 2 * core
    opposite = (me + 8) % CTX
    x_right = yhi * 8 + 2 * ((xpos + 1) % 4) + core
    x_left = yhi * 8 + 2 * ((xpos + 3) % 4) + core
    z_right = ylo * PLANE + (zpos + 1) % PLANE
    z_left = ylo * PLANE + (zpos + PLANE - 1) % PLANE
    y_other = (1 - ylo) * PLANE + zpos
    same = ylo == core
    crossed = ylo != core

    def remote(src, dst, send, recv, **target):
        return pltpu.make_async_remote_copy(
            src_ref=src, dst_ref=dst, send_sem=send, recv_sem=recv,
            device_id=target, device_id_type=MESH,
        )

    table_copy = pltpu.make_async_copy(table_hbm, table, local_sem.at[0])
    table_copy.start()
    w_copy = pltpu.make_async_copy(w_hbm, w, local_sem.at[1])

    @pl.when(same)
    def _():
        w_copy.start()

    barrier = pltpu.get_barrier_semaphore()
    for k in range(1, CTX):
        pl.semaphore_signal(
            barrier, inc=1, device_id={"ctx": (me + k) % CTX}, device_id_type=MESH
        )
    for other in (z_right, z_left):
        pl.semaphore_signal(barrier, inc=1, device_id={"mp": other}, device_id_type=MESH)
    for other in (sibling, (sibling + 8) % CTX):
        pl.semaphore_signal(
            barrier, inc=1, device_id={"ctx": other, "mp": y_other}, device_id_type=MESH
        )
    pl.semaphore_wait(barrier, CTX - 1 + 4)

    rim_copy = remote(
        ids_ref.at[:, pl.ds(rows - 128, 128)], rim, rim_sem.at[0], rim_sem.at[1],
        ctx=(me + 1) % CTX,
    )
    rim_copy.start()

    quarter = all_chans // 4

    def w_rows(j, place, shift=0, count=quarter):
        return w.at[j, pl.ds(pl.multiple_of((place % 4) * quarter + shift, 16), count), :]

    def wy_copy(j):
        at = pl.ds(pl.multiple_of(xpos * quarter, 16), quarter)
        return remote(
            w_hbm.at[j, at, :], w_rows(j, xpos), wy_send.at[j], wy_recv.at[j],
            ctx=sibling, mp=y_other,
        )

    def wx_copy(j, step, direction, outgoing):
        sign = 3 if direction == 0 else 1
        place = xpos + sign * (step - 1 if outgoing else step)
        ref = w_rows(j, place, *((0, quarter) if step == 1 else (direction * quarter // 2, quarter // 2)))
        k = (j * 2 + step - 1) * 2 + direction
        return remote(
            ref, ref, wx_send.at[k], wx_recv.at[k], ctx=x_right if direction == 0 else x_left
        )

    def w_tick(j, step):
        @pl.when(crossed)
        def _():
            if step == 0:
                wy_copy(j).wait_recv()
            for direction in (0, 1):
                if step > 0:
                    wx_copy(j, step, direction, False).wait_recv()
                if step < 2:
                    wx_copy(j, step + 1, direction, True).start()

    @pl.when(crossed)
    def _():
        for j in range(3):
            wy_copy(j).start()

    vocab = table.shape[1]

    def looked(ids, feature):
        at = lax.broadcasted_iota(jnp.int32, (vocab, ids.shape[1]), 0)
        hot = (at == ids).astype(jnp.float32).astype(jnp.bfloat16)
        return lax.dot_general(
            hot, table[feature], (((0,), (0,)), ((), ())), preferred_element_type=jnp.float32
        )

    damping = rates_ref[...] / total_len
    twice = 2.0 * damping
    small = twice * (
        1.0
        - twice
        * (
            0.5
            - twice
            * (1.0 / 6 - twice * (1.0 / 24 - twice * (1.0 / 120 - twice * (1.0 / 720))))
        )
    )
    grown = jnp.where(twice < 0.1, small, 1.0 - jnp.exp(-twice))
    mode_weight = resid_ref[...] * jnp.sqrt(grown)
    one_step = jnp.exp(-damping)
    for r in range(modes):
        decay[r] = jnp.broadcast_to(one_step[r : r + 1, :], (SEGS, chans))
        weight[r] = jnp.broadcast_to(mode_weight[r : r + 1, :], (SEGS, chans))

    table_copy.wait()
    for j in range(3):
        feats[j, 8:, :] = looked(ids_ref[...], j)
    rim_copy.wait_recv()
    for j in range(3):
        before = looked(rim[...], j)[120:128, :]
        feats[j, 0:8, :] = jnp.where(me > 0, before, 0.0)

    def smooth(j, at, count):
        total = filt_ref[0, j : j + 1, :] * feats[j, 8 + at : 8 + at + count, :]
        for tap in range(1, TAPS):
            total = total + filt_ref[tap, j : j + 1, :] * feats[
                j, 8 + at - tap : 8 + at - tap + count, :
            ]
        return total

    groups = [(g, slice(g * 128, (g + 1) * 128)) for g in range(chans // 128)]
    for at in range(0, rows, 96):
        gated = smooth(1, at, 96) * smooth(2, at, 96)
        led = smooth(0, at, 96)
        for g, lanes in groups:
            gate[g, at : at + 96, :] = gated[:, lanes]
            lead[g, at : at + 96, :] = led[:, lanes]

    for g, lanes in groups:
        fade = decay[:, :, lanes]

        def ended(i, state, g=g, fade=fade):
            row = gate[g, pl.ds(i, SEGS, stride=steps), :]
            return fade * state + row[None]

        ends[:, :, lanes] = lax.fori_loop(
            0, steps, ended, jnp.zeros((modes, SEGS, 128), jnp.float32)
        )
    segment_fade = jnp.exp(-damping * steps)
    running = jnp.zeros((modes, chans), jnp.float32)
    for j in range(SEGS):
        starts[:, j, :] = running
        running = segment_fade * running + ends[:, j, :]
    states[me] = running
    state_copies = []
    for k in range(1, CTX):
        copy = remote(
            states.at[me], states.at[me], state_send.at[k - 1], state_recv.at[k - 1],
            ctx=(me + k) % CTX,
        )
        copy.start()
        state_copies.append(copy)
    w_tick(0, 0)
    q_acc[...] = jnp.zeros_like(q_acc)
    q_max[...] = jnp.full_like(q_max, NEG_FILL)
    for k in range(1, CTX):
        source = (me + CTX - k) % CTX
        remote(
            states.at[source], states.at[source], state_send.at[k - 1], state_recv.at[k - 1],
            ctx=(me + k) % CTX,
        ).wait_recv()

    def gathered(k, total):
        gap = jnp.maximum(me - 1 - k, 0).astype(jnp.float32) * rows
        return total + jnp.where(k < me, jnp.exp(-damping * gap) * states[k], 0.0)

    incoming = lax.fori_loop(0, CTX, gathered, jnp.zeros((modes, chans), jnp.float32))
    for j in range(SEGS):
        starts[:, j, :] += jnp.exp(-damping * (steps * j)) * incoming
    w_tick(1, 0)

    for g, lanes in groups:
        fade = decay[:, :, lanes]
        skip = skip_ref[:, lanes]

        def stepped(i, state, g=g, lanes=lanes, fade=fade, skip=skip):
            at = pl.ds(i, SEGS, stride=steps)
            row = gate[g, at, :]
            state = fade * state + row[None]
            conv = jnp.sum(weight[:, :, lanes] * state, axis=0)
            gate[g, at, :] = lead[g, at, :] * (conv + skip * row)
            return state

        lax.fori_loop(0, steps, stepped, starts[:, :, lanes])
        if g == 0:
            w_tick(2, 0)
            w_tick(0, 1)

    def columns(plane, z_at):
        return pl.ds(pl.multiple_of((plane * PLANE + z_at) * chans, chans), chans)

    made_out = jnp.concatenate([gate[g] for g, _ in groups], axis=1).astype(jnp.bfloat16)
    own[...] = made_out

    @pl.when(same)
    def _():
        x[:, columns(ylo, zpos)] = own[...]

    def rows_of(n, shift=0, count=part):
        return pl.ds(pl.multiple_of(n * part + shift, 16), count)

    def y_copy(n):
        return remote(
            own.at[rows_of(n), :], x.at[rows_of(n), columns(ylo, zpos)],
            y_send.at[n], y_recv.at[n], ctx=sibling, mp=y_other,
        )

    @pl.when(crossed)
    def _():
        for n in range(CHUNKS):
            y_copy(n).start()

    hyena_copy = pltpu.make_async_copy(own, hyena_hbm, local_sem.at[2])
    hyena_copy.start()

    def z_part(n, step, direction, plane, outgoing):
        away = step - 1 if outgoing else step
        origin = (zpos + PLANE - away) % PLANE if direction == 0 else (zpos + away) % PLANE
        count, shift = (half, direction * half) if step == 4 else (part, 0)
        return x.at[rows_of(n, shift, count), columns(plane, origin)]

    def z_copy(n, step, direction, outgoing):
        ref = z_part(n, step, direction, core, outgoing)
        k = (n * 4 + step - 1) * 2 + direction
        return remote(
            ref, ref, z_send.at[k], z_recv.at[k], mp=z_right if direction == 0 else z_left
        )

    def d_copy(n, step, direction, outgoing):
        plane = core if outgoing else 1 - core
        if step == 0:
            ref = x.at[rows_of(n), columns(plane, zpos)]
        else:
            ref = z_part(n, step, direction, plane, False)
        k = n * 9 + (0 if step == 0 else 2 * step - 1 + direction)
        return remote(ref, ref, d_send.at[k], d_recv.at[k], ctx=sibling)

    d_kinds = [(0, 0)] + [(step, direction) for step in (1, 2, 3, 4) for direction in (0, 1)]

    def begin(n):
        @pl.when(crossed)
        def _():
            y_copy(n).wait_recv()

        for direction in (0, 1):
            z_copy(n, 1, direction, True).start()
        d_copy(n, 0, 0, True).start()

    def arrive(n, step):
        for direction in (0, 1):
            z_copy(n, step, direction, False).wait_recv()
            if step < 4:
                z_copy(n, step + 1, direction, True).start()
            d_copy(n, step, direction, True).start()

    def block_of(which, place, at_core):
        return which * 8 + 2 * (place % 4) + at_core

    def kv_rows(owner, n, shift=0, count=part):
        return kv.at[pl.ds(pl.multiple_of(n * span + owner * part + shift, 16), count), :]

    def home_copies(n, head):
        at = rows_of(n)
        k = (n * 2 + head) * 2
        r = (n * 2 + yhi) * 2
        target = {"ctx": block_of(head, xpos, ylo), "mp": core * PLANE + zpos}
        return (
            remote(
                kv_out.at[head, at, :], kv_rows(block_of(yhi, xpos, ylo), n),
                h_send.at[k], h_recv.at[r], **target,
            ),
            remote(
                q_out.at[head, at, :], qs.at[yhi, at, :],
                h_send.at[k + 1], h_recv.at[r + 1], **target,
            ),
        )

    def local_copies(n, head):
        at = rows_of(n)
        return (
            pltpu.make_async_copy(
                kv_out.at[head, at, :], kv_rows(block_of(yhi, xpos, ylo), n), l_sem.at[n * 2]
            ),
            pltpu.make_async_copy(
                q_out.at[head, at, :], qs.at[yhi, at, :], l_sem.at[n * 2 + 1]
            ),
        )

    def home_waits(n, which):
        at = rows_of(n)
        k = (n * 2 + which) * 2
        at_home = jnp.logical_and(same, yhi == which)

        @pl.when(at_home)
        def _():
            for copy in local_copies(n, which):
                copy.wait()

        @pl.when(jnp.logical_not(at_home))
        def _():
            target = {"ctx": block_of(which, xpos, ylo), "mp": core * PLANE + zpos}
            remote(
                kv_out.at[0, at, :], kv_rows(block_of(which, xpos, core), n),
                h_send.at[k], h_recv.at[k], **target,
            ).wait_recv()
            remote(
                q_out.at[0, at, :], qs.at[which, at, :], h_send.at[k + 1], h_recv.at[k + 1],
                **target,
            ).wait_recv()

    def ring_part(n, which, step, direction, at_core, outgoing):
        sign = 3 if direction == 0 else 1
        away = step - 1 if outgoing else step
        owner = block_of(which, xpos + sign * away, at_core)
        return kv_rows(owner, n, *((0, part) if step == 1 else (direction * half, half)))

    def ring_copy(n, which, step, direction, outgoing):
        ref = ring_part(n, which, step, direction, core, outgoing)
        k = ((n * 2 + which) * 2 + step - 1) * 2 + direction
        return remote(
            ref, ref, r_send.at[k], r_recv.at[k], ctx=x_right if direction == 0 else x_left
        )

    def core_copy(n, which, step, direction, outgoing):
        at_core = core if outgoing else 1 - core
        if step == 0:
            ref = kv_rows(block_of(which, xpos, at_core), n)
        else:
            ref = ring_part(n, which, step, direction, at_core, False)
        k = (n * 2 + which) * 5 + (0 if step == 0 else 2 * step - 1 + direction)
        return remote(ref, ref, c_send.at[k], c_recv.at[k], ctx=sibling)

    c_kinds = [(0, 0)] + [(step, direction) for step in (1, 2) for direction in (0, 1)]

    def ring_begin(n):
        for which in (0, 1):
            home_waits(n, which)
            for direction in (0, 1):
                ring_copy(n, which, 1, direction, True).start()
            core_copy(n, which, 0, 0, True).start()

    def ring_tick(n, step):
        for which in (0, 1):
            for direction in (0, 1):
                ring_copy(n, which, step, direction, False).wait_recv()
                if step == 1:
                    ring_copy(n, which, 2, direction, True).start()
                core_copy(n, which, step, direction, True).start()

    def ring_end(n):
        for which in (0, 1):
            for kind in c_kinds:
                core_copy(n, which, *kind, False).wait_recv()

    def project(n):
        for kind in d_kinds:
            d_copy(n, *kind, False).wait_recv()
        at = rows_of(n)
        wide = x[at, :].astype(jnp.float32)
        squares = jnp.sum(wide * wide, axis=1, keepdims=True)
        norm = lax.rsqrt(squares / all_chans + NORM_EPSILON)
        for j in range(3):
            scale = norm * (math.log2(math.e) / math.sqrt(HEAD_DIM)) if j == 0 else norm
            made = jnp.dot(x[at, :], w[j], preferred_element_type=jnp.float32) * scale
            made = made.astype(jnp.bfloat16)
            for head in (0, 1):
                piece = made[:, head * HEAD_DIM : (head + 1) * HEAD_DIM]
                if j == 0:
                    q_out[head, at, :] = piece
                else:
                    kv_out[head, at, (j - 1) * HEAD_DIM : j * HEAD_DIM] = piece
        for head in (0, 1):
            stays = jnp.logical_and(same, yhi == head)

            @pl.when(stays)
            def _(head=head):
                for copy in local_copies(n, head):
                    copy.start()

            @pl.when(jnp.logical_not(stays))
            def _(head=head):
                for copy in home_copies(n, head):
                    copy.start()

    ones = jnp.ones((span // 2, HEAD_DIM), jnp.bfloat16)

    def scores_of(queries, block):
        return lax.dot_general(
            queries, block[:, :HEAD_DIM], (((1,), (1,)), ((), ())),
            preferred_element_type=jnp.float32,
        )

    def masked(scores, bound):
        col = lax.broadcasted_iota(jnp.int32, scores.shape, 1)
        return jnp.where(col < bound, scores, NEG_FILL)

    def pair(q_chunk, k_chunk):
        at = rows_of(q_chunk)
        row = lax.broadcasted_iota(jnp.int32, (part, 1), 0) + 1
        extra = jnp.where(k_chunk < q_chunk, part, jnp.where(k_chunk == q_chunk, row, 0))
        bound = (2 * xpos + core) * part + extra
        base = pl.multiple_of(k_chunk * span, 16)
        low = kv[pl.ds(base, span // 2), :]
        high = kv[pl.ds(pl.multiple_of(base + span // 2, 16), span // 2), :]
        for which in (1, 0):
            queries = qs[which, at, :]
            if which == 1:
                blocks = [low, high]
                scores = [scores_of(queries, low), masked(scores_of(queries, high), bound)]
            else:
                blocks = [low]
                scores = [masked(scores_of(queries, low), bound)]
            old = q_max[which, at, :]
            new = old
            for s in scores:
                new = jnp.maximum(new, jnp.max(s, axis=1, keepdims=True))
            wide = jnp.concatenate([new] * (span // 256), axis=1)
            shrink = jnp.exp2(old - new)
            total = q_acc[which, at, :] * jnp.concatenate([shrink, shrink], axis=1)
            for s, block in zip(scores, blocks):
                weights = jnp.exp2(s - wide).astype(jnp.bfloat16)
                values = jnp.concatenate([block[:, HEAD_DIM:], ones], axis=1)
                total = total + jnp.dot(weights, values, preferred_element_type=jnp.float32)
            q_acc[which, at, :] = total
            q_max[which, at, :] = new

    def pairs(n, first, last):
        def one(i, carry):
            q_chunk = jnp.where(i < n, i, n)
            k_chunk = jnp.where(i < n, n, jnp.where(i < 2 * n, i - n, n))
            pair(q_chunk, k_chunk)
            return carry

        lax.fori_loop(first, last, one, 0)

    head_lanes = pl.ds(pl.multiple_of(yhi * HEAD_DIM, HEAD_DIM), HEAD_DIM)
    other_lanes = pl.ds(pl.multiple_of((1 - yhi) * HEAD_DIM, HEAD_DIM), HEAD_DIM)

    def o_copy(m, lanes):
        at = rows_of(m)
        return remote(
            o_out.at[1 - yhi, at, :], att.at[at, lanes], o_send.at[m], o_recv.at[m], ctx=opposite
        )

    def finish(m):
        at = rows_of(m)
        for which in (0, 1):
            done = q_acc[which, at, :HEAD_DIM] / q_acc[which, at, HEAD_DIM:]
            o_out[which, at, :] = done.astype(jnp.bfloat16)
        o_copy(m, head_lanes).start()
        att[at, head_lanes] = o_out[yhi, at, :]

    w_tick(1, 1)

    def round_of(it, carry):
        def when(n):
            return pl.when(jnp.logical_and(n >= 0, n < CHUNKS))

        def some_pairs(n, piece):
            @pl.when(jnp.logical_and(n >= 0, n < CHUNKS - 1))
            def _():
                count = 2 * n + 1
                pairs(n, count * piece // 3, count * (piece + 1) // 3)

        @when(it)
        def _():
            begin(it)

        @when(it - 2)
        def _():
            arrive(it - 2, 2)

        @when(it - 1)
        def _():
            arrive(it - 1, 1)

        @pl.when(it == 1)
        def _():
            w_tick(2, 1)

        @pl.when(it == 2)
        def _():
            w_tick(0, 2)

        some_pairs(it - 7, 2)

        @when(it - 6)
        def _():
            ring_end(it - 6)

        some_pairs(it - 6, 0)

        @when(it - 5)
        def _():
            ring_tick(it - 5, 1)

        @when(it - 3)
        def _():
            arrive(it - 3, 4)

        some_pairs(it - 6, 1)

        @when(it - 4)
        def _():
            ring_begin(it - 4)

        @pl.when(it == 3)
        def _():
            w_tick(1, 2)
            w_tick(2, 2)

            @pl.when(same)
            def _():
                w_copy.wait()

        @when(it - 3)
        def _():
            project(it - 3)

        @when(it - 5)
        def _():
            ring_tick(it - 5, 2)

        @when(it - 2)
        def _():
            arrive(it - 2, 3)

        return carry

    lax.fori_loop(0, CHUNKS + 6, round_of, 0)

    last = CHUNKS - 1

    def closing(m, carry):
        pair(m, last)
        finish(m)
        return carry

    lax.fori_loop(0, last, closing, 0)
    pairs(last, last, 2 * last + 1)
    finish(last)

    rim_copy.wait_send()
    for copy in state_copies:
        copy.wait_send()

    @pl.when(crossed)
    def _():
        for j in range(3):
            wy_copy(j).wait_send()
            for step in (1, 2):
                for direction in (0, 1):
                    wx_copy(j, step, direction, True).wait_send()

    def sent(n, carry):
        @pl.when(crossed)
        def _():
            y_copy(n).wait_send()

        for direction in (0, 1):
            for step in (1, 2, 3, 4):
                z_copy(n, step, direction, True).wait_send()
        for kind in d_kinds:
            d_copy(n, *kind, True).wait_send()
        for which in (0, 1):
            for step, direction in c_kinds:
                core_copy(n, which, step, direction, True).wait_send()
                if step > 0:
                    ring_copy(n, which, step, direction, True).wait_send()

            @pl.when(jnp.logical_not(jnp.logical_and(same, yhi == which)))
            def _(which=which):
                for copy in home_copies(n, which):
                    copy.wait_send()

        o_copy(n, head_lanes).wait_send()
        return carry

    lax.fori_loop(0, CHUNKS, sent, 0)
    hyena_copy.wait()
    for m in range(CHUNKS):
        o_copy(m, other_lanes).wait_recv()
    att_copy = pltpu.make_async_copy(att, att_hbm, local_sem.at[3])
    att_copy.start()
    att_copy.wait()


def per_device(token_ids, feature_table, short_filter, rates, residues, skip_weight, w_qkv):
    rows = token_ids.shape[0]
    vocab, _, chans = feature_table.shape
    modes = rates.shape[1]
    all_chans, _, width = w_qkv.shape
    f32, bf16 = jnp.float32, jnp.bfloat16
    dma = pltpu.SemaphoreType.DMA
    vmem = pl.BlockSpec(memory_space=pltpu.VMEM)
    hbm = pl.BlockSpec(memory_space=pl.ANY)
    return pl.pallas_call(
        mixer_kernel,
        out_shape=(
            jax.ShapeDtypeStruct((rows, chans), bf16),
            jax.ShapeDtypeStruct((rows, width), bf16),
        ),
        in_specs=[vmem, hbm, vmem, vmem, vmem, vmem, hbm],
        out_specs=(hbm, hbm),
        scratch_shapes=[
            pltpu.VMEM((3, vocab, chans), bf16),
            pltpu.VMEM((3, all_chans, width), bf16),
            pltpu.VMEM((3, 8 + rows, chans), f32),
            pltpu.VMEM((chans // 128, rows, 128), f32),
            pltpu.VMEM((chans // 128, rows, 128), f32),
            pltpu.VMEM((1, 128), jnp.int32),
            pltpu.VMEM((modes, SEGS, chans), f32),
            pltpu.VMEM((modes, SEGS, chans), f32),
            pltpu.VMEM((modes, SEGS, chans), f32),
            pltpu.VMEM((modes, SEGS, chans), f32),
            pltpu.VMEM((CTX, modes, chans), f32),
            pltpu.VMEM((rows, chans), bf16),
            pltpu.VMEM((rows, all_chans), bf16),
            pltpu.VMEM((CTX * rows, 2 * HEAD_DIM), bf16),
            pltpu.VMEM((2, rows, HEAD_DIM), bf16),
            pltpu.VMEM((2, rows, 2 * HEAD_DIM), bf16),
            pltpu.VMEM((2, rows, HEAD_DIM), bf16),
            pltpu.VMEM((2, rows, 2 * HEAD_DIM), f32),
            pltpu.VMEM((2, rows, HEAD_DIM), f32),
            pltpu.VMEM((2, rows, HEAD_DIM), bf16),
            pltpu.VMEM((rows, width), bf16),
            dma((4,)),
            dma((2,)),
            dma((CTX - 1,)),
            dma((CTX - 1,)),
            dma((3,)),
            dma((3,)),
            dma((12,)),
            dma((12,)),
            dma((CHUNKS,)),
            dma((CHUNKS,)),
            dma((CHUNKS * 8,)),
            dma((CHUNKS * 8,)),
            dma((CHUNKS * 9,)),
            dma((CHUNKS * 9,)),
            dma((CHUNKS * 4,)),
            dma((CHUNKS * 4,)),
            dma((CHUNKS * 2,)),
            dma((CHUNKS * 10,)),
            dma((CHUNKS * 10,)),
            dma((CHUNKS * 8,)),
            dma((CHUNKS * 8,)),
            dma((CHUNKS,)),
            dma((CHUNKS,)),
        ],
        compiler_params=pltpu.CompilerParams(
            collective_id=0, has_side_effects=True, vmem_limit_bytes=56 * 1024 * 1024
        ),
        name="mixer",
    )(
        token_ids.reshape(1, rows),
        jnp.transpose(feature_table, (1, 0, 2)),
        short_filter,
        rates.T,
        residues.T,
        skip_weight.reshape(1, chans),
        jnp.transpose(w_qkv, (1, 0, 2)),
    )


def solution(mesh):
    in_specs = (
        P("ctx"),
        P(None, None, "mp"),
        P(None, None, "mp"),
        P("mp", None),
        P("mp", None),
        P("mp"),
        P(None, None, "mp"),
    )
    out_specs = (P("ctx", "mp"), P("ctx", "mp"))
    return jax.shard_map(
        per_device, mesh=mesh, in_specs=in_specs, out_specs=out_specs, check_vma=False
    )
```

time: 181 us -> 130 us (0.72)
  the two profiles are of different devices: /device:TPU:7 before, /device:TPU:1 now
where the time goes in v2:
time: 130 us; the launch traced here: 129 us
  Pallas kernels  124 us (95%)
  local copies, waits for them, and re-layouts  4.8 us (4%)
    pallas_call x1, Pallas kernels, per_device(): pl.pallas_call(mixer_kernel, out_shape=(jax.ShapeDtypeStruct((rows, chans...  124 us
    unnamed x2, local copies, waits for them, and re-layouts  3.53 us

profile of v2, /device:TPU:1, one launch (start us, length us, event | category | flops | bytes accessed | tf_op | source)
XLA Modules:
  0.0 129.3 jit_solution(16686474252065937445)
XLA Ops:
  0.6 1.3 reshape.10.ids_ref
  1.9 123.8 %mixer.1 = (bf16[768,256]{1,0:T(8,128)(2,1)}, bf16[768,256]{1,0:T(8,128)(2,1)}) custom-call(s32[1,768]{1,0:T(1,128)} %reshape.10.ids_ref, bf16[3,512,256]{2,1,0:T(8,128)(2,1)} %bitcast.6, f32[3,3,256]{2,1,0:T(4,128)} %filt_ref.1, f32[16,256]{1,0:T(8,128)} %bitcast.7, f32[16,256]{1,0:T(8,128)} %bitcast.8, f32[1,256]{1,0:T(1,128)} %bitcast.9, ...), custom_call_target="tpu_custom_call" | custom-call | tf_op jit(solution)/shard_map/mixer/pallas_call | solution.py:650
  125.7 1.8 %copy.11 = bf16[768,256]{1,0:T(8,128)(2,1)} copy(bf16[768,256]{1,0:T(8,128)(2,1)} %get-tuple-element.4) | data formatting | bytes 786432
  127.5 1.8 %copy.12 = bf16[768,256]{1,0:T(8,128)(2,1)} copy(bf16[768,256]{1,0:T(8,128)(2,1)} %get-tuple-element.5) | data formatting | bytes 786432

commit v3 on v2

--- a/solution.py
+++ b/solution.py
@@ -24,7 +24,7 @@
 def mixer_kernel(
     ids_ref, table_hbm, filt_ref, rates_ref, resid_ref, skip_ref, w_hbm,
     hyena_hbm, att_hbm,
-    table, w, feats, gate, lead, rim, decay, weight, ends, starts, states,
+    table, hot, w, feats, gate, lead, mixed, rim, decay, weight, ends, starts, states,
     own, x, kv, qs, kv_out, q_out, q_acc, q_max, o_out, att,
     local_sem, rim_sem, state_send, state_recv,
     wy_send, wy_recv, wx_send, wx_recv,
@@ -83,59 +83,65 @@
         pl.semaphore_signal(
             barrier, inc=1, device_id={"ctx": other, "mp": y_other}, device_id_type=MESH
         )
+    vocab = table.shape[1]
+    place = lax.broadcasted_iota(jnp.int32, (128, 128), 1)
+
+    def one_hot(ids_row):
+        ids = jnp.transpose(jnp.broadcast_to(ids_row, (128, 128)))
+        hits = [(ids == place + at).astype(jnp.float32) for at in range(0, vocab, 128)]
+        return jnp.concatenate(hits, axis=1).astype(jnp.bfloat16)
+
+    for r in range(rows // 128):
+        hot[r * 128 : (r + 1) * 128, :] = one_hot(ids_ref[r : r + 1, :])
+    table_copy.wait()
+    for j in range(3):
+        feats[j, 8:, :] = jnp.dot(hot[...], table[j], preferred_element_type=jnp.float32)
+
     pl.semaphore_wait(barrier, CTX - 1 + 4)
 
-    rim_copy = remote(
-        ids_ref.at[:, pl.ds(rows - 128, 128)], rim, rim_sem.at[0], rim_sem.at[1],
-        ctx=(me + 1) % CTX,
-    )
+    rim_copy = remote(ids_ref, rim, rim_sem.at[0], rim_sem.at[1], ctx=(me + 1) % CTX)
     rim_copy.start()
 
     quarter = all_chans // 4
-
-    def w_rows(j, place, shift=0, count=quarter):
-        return w.at[j, pl.ds(pl.multiple_of((place % 4) * quarter + shift, 16), count), :]
-
-    def wy_copy(j):
-        at = pl.ds(pl.multiple_of(xpos * quarter, 16), quarter)
+    piece = quarter // 2
+
+    def w_rows(i, place, shift=0, count=piece):
+        at = (place % 4) * quarter + (i % 2) * piece + shift
+        return pl.ds(pl.multiple_of(at, 16), count)
+
+    def wy_copy(i):
+        at = w_rows(i, xpos)
         return remote(
-            w_hbm.at[j, at, :], w_rows(j, xpos), wy_send.at[j], wy_recv.at[j],
-            ctx=sibling, mp=y_other,
-        )
-
-    def wx_copy(j, step, direction, outgoing):
+            w_hbm.at[i // 2, at, :], w.at[i // 2, at, :], wy_send.at[i], wy_recv.at[i],
+            ctx=sibling if i % 2 == 0 else (sibling + 8) % CTX, mp=y_other,
+        )
+
+    def wx_copy(i, step, direction, outgoing):
         sign = 3 if direction == 0 else 1
-        place = xpos + sign * (step - 1 if outgoing else step)
-        ref = w_rows(j, place, *((0, quarter) if step == 1 else (direction * quarter // 2, quarter // 2)))
-        k = (j * 2 + step - 1) * 2 + direction
+        away = sign * (step - 1 if outgoing else step)
+        cut = (0, piece) if step == 1 else (direction * piece // 2, piece // 2)
+        ref = w.at[i // 2, w_rows(i, xpos + away, *cut), :]
+        k = (i * 2 + step - 1) * 2 + direction
         return remote(
             ref, ref, wx_send.at[k], wx_recv.at[k], ctx=x_right if direction == 0 else x_left
         )
 
-    def w_tick(j, step):
+    def w_ticks(*ticks):
         @pl.when(crossed)
         def _():
-            if step == 0:
-                wy_copy(j).wait_recv()
-            for direction in (0, 1):
-                if step > 0:
-                    wx_copy(j, step, direction, False).wait_recv()
-                if step < 2:
-                    wx_copy(j, step + 1, direction, True).start()
+            for step, i in ticks:
+                if step == 0:
+                    wy_copy(i).wait_recv()
+                for direction in (0, 1):
+                    if step > 0:
+                        wx_copy(i, step, direction, False).wait_recv()
+                    if step < 2:
+                        wx_copy(i, step + 1, direction, True).start()
 
     @pl.when(crossed)
     def _():
-        for j in range(3):
-            wy_copy(j).start()
-
-    vocab = table.shape[1]
-
-    def looked(ids, feature):
-        at = lax.broadcasted_iota(jnp.int32, (vocab, ids.shape[1]), 0)
-        hot = (at == ids).astype(jnp.float32).astype(jnp.bfloat16)
-        return lax.dot_general(
-            hot, table[feature], (((0,), (0,)), ((), ())), preferred_element_type=jnp.float32
-        )
+        for i in range(6):
+            wy_copy(i).start()
 
     damping = rates_ref[...] / total_len
     twice = 2.0 * damping
@@ -155,14 +161,6 @@
         decay[r] = jnp.broadcast_to(one_step[r : r + 1, :], (SEGS, chans))
         weight[r] = jnp.broadcast_to(mode_weight[r : r + 1, :], (SEGS, chans))
 
-    table_copy.wait()
-    for j in range(3):
-        feats[j, 8:, :] = looked(ids_ref[...], j)
-    rim_copy.wait_recv()
-    for j in range(3):
-        before = looked(rim[...], j)[120:128, :]
-        feats[j, 0:8, :] = jnp.where(me > 0, before, 0.0)
-
     def smooth(j, at, count):
         total = filt_ref[0, j : j + 1, :] * feats[j, 8 + at : 8 + at + count, :]
         for tap in range(1, TAPS):
@@ -172,13 +170,22 @@
         return total
 
     groups = [(g, slice(g * 128, (g + 1) * 128)) for g in range(chans // 128)]
-    for at in range(0, rows, 96):
+    def smooth_all(at):
         gated = smooth(1, at, 96) * smooth(2, at, 96)
         led = smooth(0, at, 96)
         for g, lanes in groups:
             gate[g, at : at + 96, :] = gated[:, lanes]
             lead[g, at : at + 96, :] = led[:, lanes]
 
+    for at in range(96, rows, 96):
+        smooth_all(at)
+    rim_copy.wait_recv()
+    before_hot = one_hot(rim[rows // 128 - 1 : rows // 128, :])[112:128, :]
+    for j in range(3):
+        before = jnp.dot(before_hot, table[j], preferred_element_type=jnp.float32)[8:16, :]
+        feats[j, 0:8, :] = jnp.where(me > 0, before, 0.0)
+    smooth_all(0)
+
     for g, lanes in groups:
         fade = decay[:, :, lanes]
 
@@ -187,7 +194,7 @@
             return fade * state + row[None]
 
         ends[:, :, lanes] = lax.fori_loop(
-            0, steps, ended, jnp.zeros((modes, SEGS, 128), jnp.float32)
+            0, steps, ended, jnp.zeros((modes, SEGS, 128), jnp.float32), unroll=4
         )
     segment_fade = jnp.exp(-damping * steps)
     running = jnp.zeros((modes, chans), jnp.float32)
@@ -195,32 +202,36 @@
         starts[:, j, :] = running
         running = segment_fade * running + ends[:, j, :]
     states[me] = running
-    state_copies = []
+
+    def state_copy(k, owner):
+        ref = states.at[owner]
+        return remote(
+            ref, ref, state_send.at[k - 1], state_recv.at[k - 1], ctx=(me + k) % CTX
+        )
+
     for k in range(1, CTX):
-        copy = remote(
-            states.at[me], states.at[me], state_send.at[k - 1], state_recv.at[k - 1],
-            ctx=(me + k) % CTX,
-        )
-        copy.start()
-        state_copies.append(copy)
-    w_tick(0, 0)
+
+        @pl.when(me + k < CTX)
+        def _(k=k):
+            state_copy(k, me).start()
+
+    w_ticks((0, 0), (0, 1))
     q_acc[...] = jnp.zeros_like(q_acc)
     q_max[...] = jnp.full_like(q_max, NEG_FILL)
     for k in range(1, CTX):
-        source = (me + CTX - k) % CTX
-        remote(
-            states.at[source], states.at[source], state_send.at[k - 1], state_recv.at[k - 1],
-            ctx=(me + k) % CTX,
-        ).wait_recv()
+
+        @pl.when(me >= k)
+        def _(k=k):
+            state_copy(k, (me + CTX - k) % CTX).wait_recv()
 
     def gathered(k, total):
-        gap = jnp.maximum(me - 1 - k, 0).astype(jnp.float32) * rows
-        return total + jnp.where(k < me, jnp.exp(-damping * gap) * states[k], 0.0)
-
-    incoming = lax.fori_loop(0, CTX, gathered, jnp.zeros((modes, chans), jnp.float32))
+        gap = (me - 1 - k).astype(jnp.float32) * rows
+        return total + jnp.exp(-damping * gap) * states[k]
+
+    incoming = lax.fori_loop(0, me, gathered, jnp.zeros((modes, chans), jnp.float32))
     for j in range(SEGS):
         starts[:, j, :] += jnp.exp(-damping * (steps * j)) * incoming
-    w_tick(1, 0)
+    w_ticks((0, 2), (0, 3))
 
     for g, lanes in groups:
         fade = decay[:, :, lanes]
@@ -231,18 +242,15 @@
             row = gate[g, at, :]
             state = fade * state + row[None]
             conv = jnp.sum(weight[:, :, lanes] * state, axis=0)
-            gate[g, at, :] = lead[g, at, :] * (conv + skip * row)
+            mixed[g, at, :] = lead[g, at, :] * (conv + skip * row)
             return state
 
-        lax.fori_loop(0, steps, stepped, starts[:, :, lanes])
-        if g == 0:
-            w_tick(2, 0)
-            w_tick(0, 1)
+        lax.fori_loop(0, steps, stepped, starts[:, :, lanes], unroll=2)
 
     def columns(plane, z_at):
         return pl.ds(pl.multiple_of((plane * PLANE + z_at) * chans, chans), chans)
 
-    made_out = jnp.concatenate([gate[g] for g, _ in groups], axis=1).astype(jnp.bfloat16)
+    made_out = jnp.concatenate([mixed[g] for g, _ in groups], axis=1).astype(jnp.bfloat16)
     own[...] = made_out
 
     @pl.when(same)
@@ -265,6 +273,7 @@
 
     hyena_copy = pltpu.make_async_copy(own, hyena_hbm, local_sem.at[2])
     hyena_copy.start()
+    w_ticks((1, 0))
 
     def z_part(n, step, direction, plane, outgoing):
         away = step - 1 if outgoing else step
@@ -279,16 +288,11 @@
             ref, ref, z_send.at[k], z_recv.at[k], mp=z_right if direction == 0 else z_left
         )
 
-    def d_copy(n, step, direction, outgoing):
+    def d_copy(n, outgoing):
         plane = core if outgoing else 1 - core
-        if step == 0:
-            ref = x.at[rows_of(n), columns(plane, zpos)]
-        else:
-            ref = z_part(n, step, direction, plane, False)
-        k = n * 9 + (0 if step == 0 else 2 * step - 1 + direction)
-        return remote(ref, ref, d_send.at[k], d_recv.at[k], ctx=sibling)
-
-    d_kinds = [(0, 0)] + [(step, direction) for step in (1, 2, 3, 4) for direction in (0, 1)]
+        width = PLANE * chans
+        ref = x.at[rows_of(n), pl.ds(pl.multiple_of(plane * width, width), width)]
+        return remote(ref, ref, d_send.at[n], d_recv.at[n], ctx=sibling)
 
     def begin(n):
         @pl.when(crossed)
@@ -297,20 +301,20 @@
 
         for direction in (0, 1):
             z_copy(n, 1, direction, True).start()
-        d_copy(n, 0, 0, True).start()
 
     def arrive(n, step):
         for direction in (0, 1):
             z_copy(n, step, direction, False).wait_recv()
             if step < 4:
                 z_copy(n, step + 1, direction, True).start()
-            d_copy(n, step, direction, True).start()
+        if step == 4:
+            d_copy(n, True).start()
 
     def block_of(which, place, at_core):
-        return which * 8 + 2 * (place % 4) + at_core
-
-    def kv_rows(owner, n, shift=0, count=part):
-        return kv.at[pl.ds(pl.multiple_of(n * span + owner * part + shift, 16), count), :]
+        return which * 8 + 2 * place + at_core
+
+    def kv_home(which, at_core, n):
+        return kv.at[n, which, at_core, xpos]
 
     def home_copies(n, head):
         at = rows_of(n)
@@ -319,7 +323,7 @@
         target = {"ctx": block_of(head, xpos, ylo), "mp": core * PLANE + zpos}
         return (
             remote(
-                kv_out.at[head, at, :], kv_rows(block_of(yhi, xpos, ylo), n),
+                kv_out.at[head, at, :], kv_home(yhi, ylo, n),
                 h_send.at[k], h_recv.at[r], **target,
             ),
             remote(
@@ -332,7 +336,7 @@
         at = rows_of(n)
         return (
             pltpu.make_async_copy(
-                kv_out.at[head, at, :], kv_rows(block_of(yhi, xpos, ylo), n), l_sem.at[n * 2]
+                kv_out.at[head, at, :], kv_home(yhi, ylo, n), l_sem.at[n * 2]
             ),
             pltpu.make_async_copy(
                 q_out.at[head, at, :], qs.at[yhi, at, :], l_sem.at[n * 2 + 1]
@@ -353,7 +357,7 @@
         def _():
             target = {"ctx": block_of(which, xpos, ylo), "mp": core * PLANE + zpos}
             remote(
-                kv_out.at[0, at, :], kv_rows(block_of(which, xpos, core), n),
+                kv_out.at[0, at, :], kv_home(which, core, n),
                 h_send.at[k], h_recv.at[k], **target,
             ).wait_recv()
             remote(
@@ -361,53 +365,39 @@
                 **target,
             ).wait_recv()
 
-    def ring_part(n, which, step, direction, at_core, outgoing):
+    def ring_copy(n, step, direction, outgoing):
         sign = 3 if direction == 0 else 1
         away = step - 1 if outgoing else step
-        owner = block_of(which, xpos + sign * away, at_core)
-        return kv_rows(owner, n, *((0, part) if step == 1 else (direction * half, half)))
-
-    def ring_copy(n, which, step, direction, outgoing):
-        ref = ring_part(n, which, step, direction, core, outgoing)
-        k = ((n * 2 + which) * 2 + step - 1) * 2 + direction
+        at = slice(0, part) if step == 1 else slice(direction * half, direction * half + half)
+        ref = kv.at[n, :, core, (xpos + sign * away) % 4, at, :]
+        k = (n * 2 + step - 1) * 2 + direction
         return remote(
             ref, ref, r_send.at[k], r_recv.at[k], ctx=x_right if direction == 0 else x_left
         )
 
-    def core_copy(n, which, step, direction, outgoing):
-        at_core = core if outgoing else 1 - core
-        if step == 0:
-            ref = kv_rows(block_of(which, xpos, at_core), n)
-        else:
-            ref = ring_part(n, which, step, direction, at_core, False)
-        k = (n * 2 + which) * 5 + (0 if step == 0 else 2 * step - 1 + direction)
-        return remote(ref, ref, c_send.at[k], c_recv.at[k], ctx=sibling)
-
-    c_kinds = [(0, 0)] + [(step, direction) for step in (1, 2) for direction in (0, 1)]
+    def core_copy(n, outgoing):
+        ref = kv.at[n, :, core if outgoing else 1 - core]
+        return remote(ref, ref, c_send.at[n], c_recv.at[n], ctx=sibling)
 
     def ring_begin(n):
         for which in (0, 1):
             home_waits(n, which)
-            for direction in (0, 1):
-                ring_copy(n, which, 1, direction, True).start()
-            core_copy(n, which, 0, 0, True).start()
+        for direction in (0, 1):
+            ring_copy(n, 1, direction, True).start()
 
     def ring_tick(n, step):
-        for which in (0, 1):
-            for direction in (0, 1):
-                ring_copy(n, which, step, direction, False).wait_recv()
-                if step == 1:
-                    ring_copy(n, which, 2, direction, True).start()
-                core_copy(n, which, step, direction, True).start()
+        for direction in (0, 1):
+            ring_copy(n, step, direction, False).wait_recv()
+            if step == 1:
+                ring_copy(n, 2, direction, True).start()
+        if step == 2:
+            core_copy(n, True).start()
 
     def ring_end(n):
-        for which in (0, 1):
-            for kind in c_kinds:
-                core_copy(n, which, *kind, False).wait_recv()
+        core_copy(n, False).wait_recv()
 
     def project(n):
-        for kind in d_kinds:
-            d_copy(n, *kind, False).wait_recv()
+        d_copy(n, False).wait_recv()
         at = rows_of(n)
         wide = x[at, :].astype(jnp.float32)
         squares = jnp.sum(wide * wide, axis=1, keepdims=True)
@@ -443,26 +433,35 @@
             preferred_element_type=jnp.float32,
         )
 
-    def masked(scores, bound):
-        col = lax.broadcasted_iota(jnp.int32, scores.shape, 1)
-        return jnp.where(col < bound, scores, NEG_FILL)
+    def masked(scores, bounds):
+        width = scores.shape[1] // 2
+        col = lax.broadcasted_iota(jnp.int32, (part, width), 1)
+        return jnp.concatenate(
+            [
+                jnp.where(col < bound, scores[:, i * width : (i + 1) * width], NEG_FILL)
+                for i, bound in enumerate(bounds)
+            ],
+            axis=1,
+        )
 
     def pair(q_chunk, k_chunk):
         at = rows_of(q_chunk)
         row = lax.broadcasted_iota(jnp.int32, (part, 1), 0) + 1
         extra = jnp.where(k_chunk < q_chunk, part, jnp.where(k_chunk == q_chunk, row, 0))
-        bound = (2 * xpos + core) * part + extra
-        base = pl.multiple_of(k_chunk * span, 16)
-        low = kv[pl.ds(base, span // 2), :]
-        high = kv[pl.ds(pl.multiple_of(base + span // 2, 16), span // 2), :]
+        bounds = [
+            xpos * part + jnp.where(core == 0, extra, part),
+            xpos * part + jnp.where(core == 0, 0, extra),
+        ]
+        low = kv[k_chunk, 0].reshape(span // 2, 2 * HEAD_DIM)
+        high = kv[k_chunk, 1].reshape(span // 2, 2 * HEAD_DIM)
         for which in (1, 0):
             queries = qs[which, at, :]
             if which == 1:
                 blocks = [low, high]
-                scores = [scores_of(queries, low), masked(scores_of(queries, high), bound)]
+                scores = [scores_of(queries, low), masked(scores_of(queries, high), bounds)]
             else:
                 blocks = [low]
-                scores = [masked(scores_of(queries, low), bound)]
+                scores = [masked(scores_of(queries, low), bounds)]
             old = q_max[which, at, :]
             new = old
             for s in scores:
@@ -503,8 +502,6 @@
         o_copy(m, head_lanes).start()
         att[at, head_lanes] = o_out[yhi, at, :]
 
-    w_tick(1, 1)
-
     def round_of(it, carry):
         def when(n):
             return pl.when(jnp.logical_and(n >= 0, n < CHUNKS))
@@ -515,26 +512,31 @@
                 count = 2 * n + 1
                 pairs(n, count * piece // 3, count * (piece + 1) // 3)
 
+        def w_at(at_round, *ticks):
+            @pl.when(it == at_round)
+            def _():
+                w_ticks(*ticks)
+
         @when(it)
         def _():
             begin(it)
 
+        w_at(0, (0, 4), (0, 5), (1, 1))
+        w_at(1, (1, 2))
+
         @when(it - 2)
         def _():
             arrive(it - 2, 2)
 
+        w_at(2, (2, 1), (1, 4))
+        w_at(3, (2, 4))
+
         @when(it - 1)
         def _():
             arrive(it - 1, 1)
 
-        @pl.when(it == 1)
-        def _():
-            w_tick(2, 1)
-
-        @pl.when(it == 2)
-        def _():
-            w_tick(0, 2)
-
+        w_at(1, (2, 0), (1, 3))
+        w_at(2, (2, 2))
         some_pairs(it - 7, 2)
 
         @when(it - 6)
@@ -559,8 +561,7 @@
 
         @pl.when(it == 3)
         def _():
-            w_tick(1, 2)
-            w_tick(2, 2)
+            w_ticks((2, 5))
 
             @pl.when(same)
             def _():
@@ -578,6 +579,7 @@
         def _():
             arrive(it - 2, 3)
 
+        w_at(2, (1, 5), (2, 3))
         return carry
 
     lax.fori_loop(0, CHUNKS + 6, round_of, 0)
@@ -594,16 +596,19 @@
     finish(last)
 
     rim_copy.wait_send()
-    for copy in state_copies:
-        copy.wait_send()
+    for k in range(1, CTX):
+
+        @pl.when(me + k < CTX)
+        def _(k=k):
+            state_copy(k, me).wait_send()
 
     @pl.when(crossed)
     def _():
-        for j in range(3):
-            wy_copy(j).wait_send()
+        for i in range(6):
+            wy_copy(i).wait_send()
             for step in (1, 2):
                 for direction in (0, 1):
-                    wx_copy(j, step, direction, True).wait_send()
+                    wx_copy(i, step, direction, True).wait_send()
 
     def sent(n, carry):
         @pl.when(crossed)
@@ -613,13 +618,11 @@
         for direction in (0, 1):
             for step in (1, 2, 3, 4):
                 z_copy(n, step, direction, True).wait_send()
-        for kind in d_kinds:
-            d_copy(n, *kind, True).wait_send()
+            for step in (1, 2):
+                ring_copy(n, step, direction, True).wait_send()
+        d_copy(n, True).wait_send()
+        core_copy(n, True).wait_send()
         for which in (0, 1):
-            for step, direction in c_kinds:
-                core_copy(n, which, step, direction, True).wait_send()
-                if step > 0:
-                    ring_copy(n, which, step, direction, True).wait_send()
 
             @pl.when(jnp.logical_not(jnp.logical_and(same, yhi == which)))
             def _(which=which):
@@ -636,6 +639,11 @@
     att_copy = pltpu.make_async_copy(att, att_hbm, local_sem.at[3])
     att_copy.start()
     att_copy.wait()
+
+
+def hand_over(a_ref, b_ref, a_out, b_out):
+    a_out[...] = a_ref[...]
+    b_out[...] = b_ref[...]
 
 
 def per_device(token_ids, feature_table, short_filter, rates, residues, skip_weight, w_qkv):
@@ -647,7 +655,7 @@
     dma = pltpu.SemaphoreType.DMA
     vmem = pl.BlockSpec(memory_space=pltpu.VMEM)
     hbm = pl.BlockSpec(memory_space=pl.ANY)
-    return pl.pallas_call(
+    made = pl.pallas_call(
         mixer_kernel,
         out_shape=(
             jax.ShapeDtypeStruct((rows, chans), bf16),
@@ -657,11 +665,13 @@
         out_specs=(hbm, hbm),
         scratch_shapes=[
             pltpu.VMEM((3, vocab, chans), bf16),
+            pltpu.VMEM((rows, vocab), bf16),
             pltpu.VMEM((3, all_chans, width), bf16),
             pltpu.VMEM((3, 8 + rows, chans), f32),
             pltpu.VMEM((chans // 128, rows, 128), f32),
             pltpu.VMEM((chans // 128, rows, 128), f32),
-            pltpu.VMEM((1, 128), jnp.int32),
+            pltpu.VMEM((chans // 128, rows, 128), f32),
+            pltpu.VMEM((rows // 128, 128), jnp.int32),
             pltpu.VMEM((modes, SEGS, chans), f32),
             pltpu.VMEM((modes, SEGS, chans), f32),
             pltpu.VMEM((modes, SEGS, chans), f32),
@@ -669,7 +679,7 @@
             pltpu.VMEM((CTX, modes, chans), f32),
             pltpu.VMEM((rows, chans), bf16),
             pltpu.VMEM((rows, all_chans), bf16),
-            pltpu.VMEM((CTX * rows, 2 * HEAD_DIM), bf16),
+            pltpu.VMEM((CHUNKS, 2, 2, 4, rows // CHUNKS, 2 * HEAD_DIM), bf16),
             pltpu.VMEM((2, rows, HEAD_DIM), bf16),
             pltpu.VMEM((2, rows, 2 * HEAD_DIM), bf16),
             pltpu.VMEM((2, rows, HEAD_DIM), bf16),
@@ -681,23 +691,23 @@
             dma((2,)),
             dma((CTX - 1,)),
             dma((CTX - 1,)),
-            dma((3,)),
-            dma((3,)),
-            dma((12,)),
-            dma((12,)),
+            dma((6,)),
+            dma((6,)),
+            dma((24,)),
+            dma((24,)),
             dma((CHUNKS,)),
             dma((CHUNKS,)),
             dma((CHUNKS * 8,)),
             dma((CHUNKS * 8,)),
-            dma((CHUNKS * 9,)),
-            dma((CHUNKS * 9,)),
+            dma((CHUNKS,)),
+            dma((CHUNKS,)),
             dma((CHUNKS * 4,)),
             dma((CHUNKS * 4,)),
             dma((CHUNKS * 2,)),
-            dma((CHUNKS * 10,)),
-            dma((CHUNKS * 10,)),
-            dma((CHUNKS * 8,)),
-            dma((CHUNKS * 8,)),
+            dma((CHUNKS,)),
+            dma((CHUNKS,)),
+            dma((CHUNKS * 4,)),
+            dma((CHUNKS * 4,)),
             dma((CHUNKS,)),
             dma((CHUNKS,)),
         ],
@@ -706,7 +716,7 @@
         ),
         name="mixer",
     )(
-        token_ids.reshape(1, rows),
+        token_ids.reshape(rows // 128, 128),
         jnp.transpose(feature_table, (1, 0, 2)),
         short_filter,
         rates.T,
@@ -714,6 +724,14 @@
         skip_weight.reshape(1, chans),
         jnp.transpose(w_qkv, (1, 0, 2)),
     )
+    return pl.pallas_call(
+        hand_over,
+        out_shape=tuple(jax.ShapeDtypeStruct(a.shape, a.dtype) for a in made),
+        grid=(2,),
+        in_specs=[pl.BlockSpec((rows // 2, a.shape[1]), lambda i: (i, 0)) for a in made],
+        out_specs=tuple(pl.BlockSpec((rows // 2, a.shape[1]), lambda i: (i, 0)) for a in made),
+        name="hand_over",
+    )(*made)
 
 
 def solution(mesh):

time: 130 us -> 118 us (0.908)
  Pallas kernels: 124 us -> 117 us
  local copies, waits for them, and re-layouts: 4.8 us -> 0 us
    pallas_call x1, Pallas kernels: 124 us -> 115 us  [per_device(): pl.pallas_call(mixer_kernel, out_shape=(jax.ShapeDtypeStruct((rows, chans...]
    unnamed x2 -> x0, local copies, waits for them, and re-layouts: 3.53 us -> none
    pallas_call x0 -> x1, Pallas kernels: none -> 2 us  [per_device(): pl.pallas_call(hand_over, out_shape=tuple((jax.ShapeDtypeStruct(a.shape,...]
where the time goes in v3:
time: 118 us
  Pallas kernels  117 us (99%)
    pallas_call x1, Pallas kernels, per_device(): pl.pallas_call(mixer_kernel, out_shape=(jax.ShapeDtypeStruct((rows, chans...  115 us

profile of v3, /device:TPU:1, one launch (start us, length us, event | category | flops | bytes accessed | tf_op | source)
XLA Modules:
  0.0 117.8 jit_solution(7027034681753217505)
XLA Ops:
  0.6 115.1 %mixer.1 = (bf16[768,256]{1,0:T(8,128)(2,1)}, bf16[768,256]{1,0:T(8,128)(2,1)}) custom-call(s32[6,128]{1,0:T(8,128)} %bitcast.10, bf16[3,512,256]{2,1,0:T(8,128)(2,1)} %bitcast.7, f32[3,3,256]{2,1,0:T(4,128)} %filt_ref.1, f32[16,256]{1,0:T(8,128)} %bitcast.8, f32[16,256]{1,0:T(8,128)} %bitcast.9, f32[1,256]{1,0:T(1,128)} %bitcast.11, ...), custom_call_target="tpu_custom_call" | custom-call | tf_op jit(solution)/shard_map/mixer/pallas_call | solution.py:658
  115.8 2.0 %hand_over.1 = (bf16[768,256]{1,0:T(8,128)(2,1)}, bf16[768,256]{1,0:T(8,128)(2,1)}) custom-call(bf16[768,256]{1,0:T(8,128)(2,1)} %get-tuple-element.4.a_ref, bf16[768,256]{1,0:T(8,128)(2,1)} %get-tuple-element.5.b_ref), custom_call_target="tpu_custom_call" | custom-call | tf_op jit(solution)/shard_map/hand_over/pallas_call | solution.py:727

commit v4 on v3

--- a/solution.py
+++ b/solution.py
@@ -476,11 +476,16 @@
             q_acc[which, at, :] = total
             q_max[which, at, :] = new
 
-    def pairs(n, first, last):
+    def early_pairs(n, first, last):
         def one(i, carry):
-            q_chunk = jnp.where(i < n, i, n)
-            k_chunk = jnp.where(i < n, n, jnp.where(i < 2 * n, i - n, n))
-            pair(q_chunk, k_chunk)
+            pair(n, i)
+            return carry
+
+        lax.fori_loop(first, last, one, 0)
+
+    def late_pairs(n, first, last):
+        def one(i, carry):
+            pair(i, n)
             return carry
 
         lax.fori_loop(first, last, one, 0)
@@ -506,11 +511,16 @@
         def when(n):
             return pl.when(jnp.logical_and(n >= 0, n < CHUNKS))
 
-        def some_pairs(n, piece):
+        def some_early(n, piece):
+            @when(n)
+            def _():
+                early_pairs(n, n * piece // 2, n * (piece + 1) // 2)
+
+        def some_late(n, piece):
             @pl.when(jnp.logical_and(n >= 0, n < CHUNKS - 1))
             def _():
-                count = 2 * n + 1
-                pairs(n, count * piece // 3, count * (piece + 1) // 3)
+                count = n + 1
+                late_pairs(n, count * piece // 3, count * (piece + 1) // 3)
 
         def w_at(at_round, *ticks):
             @pl.when(it == at_round)
@@ -537,13 +547,13 @@
 
         w_at(1, (2, 0), (1, 3))
         w_at(2, (2, 2))
-        some_pairs(it - 7, 2)
+        some_late(it - 7, 2)
 
         @when(it - 6)
         def _():
             ring_end(it - 6)
 
-        some_pairs(it - 6, 0)
+        some_late(it - 6, 0)
 
         @when(it - 5)
         def _():
@@ -553,11 +563,13 @@
         def _():
             arrive(it - 3, 4)
 
-        some_pairs(it - 6, 1)
+        some_late(it - 6, 1)
 
         @when(it - 4)
         def _():
             ring_begin(it - 4)
+
+        some_early(it - 4, 0)
 
         @pl.when(it == 3)
         def _():
@@ -570,6 +582,8 @@
         @when(it - 3)
         def _():
             project(it - 3)
+
+        some_early(it - 5, 1)
 
         @when(it - 5)
         def _():
@@ -591,9 +605,7 @@
         finish(m)
         return carry
 
-    lax.fori_loop(0, last, closing, 0)
-    pairs(last, last, 2 * last + 1)
-    finish(last)
+    lax.fori_loop(0, CHUNKS, closing, 0)
 
     rim_copy.wait_send()
     for k in range(1, CTX):

time: 118 us -> 114 us (0.966)
  Pallas kernels: 117 us -> 113 us
    pallas_call x1, Pallas kernels: 115 us -> 111 us  [per_device(): pl.pallas_call(mixer_kernel, out_shape=(jax.ShapeDtypeStruct((rows, chans...]
where the time goes in v4:
time: 114 us; the launch traced here: 113 us
  Pallas kernels  113 us (99%)
    pallas_call x1, Pallas kernels, per_device(): pl.pallas_call(mixer_kernel, out_shape=(jax.ShapeDtypeStruct((rows, chans...  111 us

profile of v4, /device:TPU:1, one launch (start us, length us, event | category | flops | bytes accessed | tf_op | source)
XLA Modules:
  0.0 113.5 jit_solution(17374823796724846996)
XLA Ops:
  0.6 110.8 %mixer.1 = (bf16[768,256]{1,0:T(8,128)(2,1)}, bf16[768,256]{1,0:T(8,128)(2,1)}) custom-call(s32[6,128]{1,0:T(8,128)} %bitcast.10, bf16[3,512,256]{2,1,0:T(8,128)(2,1)} %bitcast.7, f32[3,3,256]{2,1,0:T(4,128)} %filt_ref.1, f32[16,256]{1,0:T(8,128)} %bitcast.8, f32[16,256]{1,0:T(8,128)} %bitcast.9, f32[1,256]{1,0:T(1,128)} %bitcast.11, ...), custom_call_target="tpu_custom_call" | custom-call | tf_op jit(solution)/shard_map/mixer/pallas_call | solution.py:670
  111.5 2.0 %hand_over.1 = (bf16[768,256]{1,0:T(8,128)(2,1)}, bf16[768,256]{1,0:T(8,128)(2,1)}) custom-call(bf16[768,256]{1,0:T(8,128)(2,1)} %get-tuple-element.4.a_ref, bf16[768,256]{1,0:T(8,128)(2,1)} %get-tuple-element.5.b_ref), custom_call_target="tpu_custom_call" | custom-call | tf_op jit(solution)/shard_map/hand_over/pallas_call | solution.py:739

commit v5 on v4

--- a/solution.py
+++ b/solution.py
@@ -607,6 +607,11 @@
 
     lax.fori_loop(0, CHUNKS, closing, 0)
 
+    for m in range(CHUNKS):
+        o_copy(m, other_lanes).wait_recv()
+    att_copy = pltpu.make_async_copy(att, att_hbm, local_sem.at[3])
+    att_copy.start()
+
     rim_copy.wait_send()
     for k in range(1, CTX):
 
@@ -646,10 +651,6 @@
 
     lax.fori_loop(0, CHUNKS, sent, 0)
     hyena_copy.wait()
-    for m in range(CHUNKS):
-        o_copy(m, other_lanes).wait_recv()
-    att_copy = pltpu.make_async_copy(att, att_hbm, local_sem.at[3])
-    att_copy.start()
     att_copy.wait()
 
 

time: 114 us -> 114 us (level)
  no operation moved by 1% of the time
where the time goes in v5:
time: 114 us; the launch traced here: 113 us
  Pallas kernels  113 us (99%)
    pallas_call x1, Pallas kernels, per_device(): pl.pallas_call(mixer_kernel, out_shape=(jax.ShapeDtypeStruct((rows, chans...  111 us

profile of v5, /device:TPU:1, one launch (start us, length us, event | category | flops | bytes accessed | tf_op | source)
XLA Modules:
  0.0 113.5 jit_solution(14406386768915331820)
XLA Ops:
  0.6 110.8 %mixer.1 = (bf16[768,256]{1,0:T(8,128)(2,1)}, bf16[768,256]{1,0:T(8,128)(2,1)}) custom-call(s32[6,128]{1,0:T(8,128)} %bitcast.10, bf16[3,512,256]{2,1,0:T(8,128)(2,1)} %bitcast.7, f32[3,3,256]{2,1,0:T(4,128)} %filt_ref.1, f32[16,256]{1,0:T(8,128)} %bitcast.8, f32[16,256]{1,0:T(8,128)} %bitcast.9, f32[1,256]{1,0:T(1,128)} %bitcast.11, ...), custom_call_target="tpu_custom_call" | custom-call | tf_op jit(solution)/shard_map/mixer/pallas_call | solution.py:671
  111.5 2.0 %hand_over.1 = (bf16[768,256]{1,0:T(8,128)(2,1)}, bf16[768,256]{1,0:T(8,128)(2,1)}) custom-call(bf16[768,256]{1,0:T(8,128)(2,1)} %get-tuple-element.4.a_ref, bf16[768,256]{1,0:T(8,128)(2,1)} %get-tuple-element.5.b_ref), custom_call_target="tpu_custom_call" | custom-call | tf_op jit(solution)/shard_map/hand_over/pallas_call | solution.py:740
